TPU v7x, 128 devices: a whole 4x4x4 slice. The times are simulated.
128 devices in a mesh: chan: 16 (over y, z_lo, core), sub: 8 (over x, z_hi).
Axes of the slice: x: 4, y: 4, z: 4 (z_hi: 2, z_lo: 2; z = z_hi * 2 + z_lo), core: 2. Of those that a mesh axis runs over, the one named last changes fastest.
Arguments:
- spectra: bfloat16 [8, 2, 512, 32768], P('sub', None, None, 'chan'), may hold values from -12 to 12
- filter_init: float32 [2, 32768], P(None, 'chan'), may hold values from -2.1 to 2.1
- profile_init: float32 [2, 512], replicated, may hold values from -1.4 to 1.4
Outputs:
- filter_out: float32 [2, 32768], P(None, 'chan')
- profile_out: float32 [2, 512], replicated
- misfit: float32 [1], replicated
All inputs are finite; a program needn't handle non-finite values.
Results may differ from a plain program's by a relative error of at most 0.0003.
Values sent between devices are 32-bit elements; how exact they have to be, the bound alone decides.
No kernel may reach another device: no remote copies, remote signals or barrier semaphores. Data moves between devices by JAX's collectives and lax.ppermute only.
A program may use at most 128 MiB of HBM per device.

v0:
```python
import jax
import jax.numpy as jnp
from jax import lax
from jax.sharding import PartitionSpec as P

CHANNELS = 32768


filter_rate = 0.1
profile_rate = 0.1
epsilon = 1e-06


def with_halo(block, sides, width):
    for axis, dim in sides:
        count = lax.axis_size(axis)
        forward = [(i, i + 1) for i in range(count - 1)]
        backward = [(target, source) for source, target in forward]
        low = lax.ppermute(
            lax.slice_in_dim(block, block.shape[dim] - width, None, axis=dim), axis, forward
        )
        high = lax.ppermute(lax.slice_in_dim(block, 0, width, axis=dim), axis, backward)
        block = jnp.concatenate([low, block, high], axis=dim)
    return block


def passed_along(block, axis, distance):
    devices = range(lax.axis_size(axis))
    route = [(i - distance, i) for i in devices if i - distance in devices]
    return lax.ppermute(block, axis, route)


def shifted_rows(values, start, shift_step, length):
    leading = values.shape[:-2]
    row_count = values.shape[-2]
    row_len = values.shape[-1]
    row_span = row_len + shift_step
    flattened = values.reshape(leading + (row_count * row_len,))
    padding = max(0, start + row_count * row_span - row_count * row_len)
    if padding > 0:
        flattened = jnp.pad(flattened, [(0, 0)] * len(leading) + [(0, padding)])
    flattened = lax.slice_in_dim(flattened, start, start + row_count * row_span, axis=len(leading))
    return flattened.reshape(leading + (row_count, row_span))[..., :length]


def filter_rows(padded, start, shift_step, length, count):
    copies = jnp.broadcast_to(padded[:, None, :], (padded.shape[0], count, padded.shape[1]))
    return shifted_rows(copies, start, shift_step, length)


def diagonal_sum(terms):
    padded_terms = jnp.pad(terms, ((0, 0), (0, 0), (0, terms.shape[1])))
    return jnp.sum(shifted_rows(padded_terms, 0, -1, terms.shape[2] + terms.shape[1] - 1), axis=1)


def on_device(spectra, filter_init, profile_init):
    harmonics = profile_init.shape[1]
    owned = filter_init.shape[1]
    local_subs = spectra.shape[0]
    block_size = min(128, harmonics)
    weight = 1.0 / (lax.axis_size("sub") * local_subs * harmonics)
    factor = -2.0 * weight
    filter_now = filter_init
    profile_now = profile_init
    padded = with_halo(filter_now, (("chan", 1),), harmonics)
    error_sum = jnp.zeros((), jnp.float32)
    profile_parts = []
    upper_ext = jnp.zeros((2, owned + harmonics), jnp.float32)
    lower_ext = jnp.zeros((2, owned + harmonics), jnp.float32)
    for block_start in range(0, harmonics, block_size):
        forward = filter_rows(padded, harmonics + block_start, 1, owned, block_size)
        backward = filter_rows(padded, harmonics - block_start, -1, owned, block_size)
        prof_re = profile_now[0, block_start : block_start + block_size][:, None]
        prof_im = profile_now[1, block_start : block_start + block_size][:, None]
        prod_re = forward[0] * backward[0] + forward[1] * backward[1]
        prod_im = forward[1] * backward[0] - forward[0] * backward[1]
        model_re = prod_re * prof_re - prod_im * prof_im
        model_im = prod_re * prof_im + prod_im * prof_re
        spectrum = spectra[0, :, block_start : block_start + block_size].astype(jnp.float32)
        resid_re = spectrum[0] - model_re
        resid_im = spectrum[1] - model_im
        error_sum = error_sum + jnp.sum(resid_re * resid_re + resid_im * resid_im)
        grad_re = jnp.sum(resid_re * prod_re + resid_im * prod_im, axis=1)
        grad_im = jnp.sum(resid_im * prod_re - resid_re * prod_im, axis=1)
        left_re = resid_re * backward[0] - resid_im * backward[1]
        left_im = resid_re * backward[1] + resid_im * backward[0]
        upper_term = jnp.stack(
            [left_re * prof_re + left_im * prof_im, left_im * prof_re - left_re * prof_im]
        )
        right_re = resid_re * forward[0] + resid_im * forward[1]
        right_im = resid_re * forward[1] - resid_im * forward[0]
        lower_term = jnp.stack(
            [right_re * prof_re - right_im * prof_im, right_re * prof_im + right_im * prof_re]
        )
        span_len = owned + block_size - 1
        upper_ext = upper_ext.at[:, block_start : block_start + span_len].add(
            diagonal_sum(upper_term)
        )
        lower_start = harmonics - block_start - block_size + 1
        lower_ext = lower_ext.at[:, lower_start : lower_start + span_len].add(
            diagonal_sum(lower_term[:, ::-1])
        )
        profile_parts.append(factor * jnp.stack([grad_re, grad_im]))
    profile_local = jnp.concatenate(profile_parts, axis=1)
    from_below = passed_along(upper_ext[:, owned:], "chan", 1)
    from_above = passed_along(lower_ext[:, :harmonics], "chan", -1)
    filter_local = upper_ext[:, :owned] + lower_ext[:, harmonics:]
    filter_local = filter_local + jnp.pad(from_below, ((0, 0), (0, owned - harmonics)))
    filter_local = filter_local + jnp.pad(from_above, ((0, 0), (owned - harmonics, 0)))
    filter_local = factor * filter_local
    filter_grad = lax.psum(filter_local, "sub")
    profile_grad, error_total = lax.psum((profile_local, error_sum), ("chan", "sub"))
    squares = lax.psum(jnp.sum(filter_grad * filter_grad), "chan")
    misfits = [error_total * weight / CHANNELS]
    filter_now = filter_now - filter_rate * filter_grad / jnp.sqrt(
        squares / (2 * CHANNELS) + epsilon
    )
    profile_now = profile_now - profile_rate * profile_grad / jnp.sqrt(
        jnp.mean(profile_grad * profile_grad) + epsilon
    )
    return (filter_now, profile_now, jnp.stack(misfits))


def solution(mesh):
    return jax.shard_map(
        on_device,
        mesh=mesh,
        in_specs=(P("sub", None, None, "chan"), P(None, "chan"), P()),
        out_specs=(P(None, "chan"), P(), P()),
        check_vma=False,
    )
```

profile of v0, /device:TPU:1, one launch (start us, length us, event | category | flops | bytes accessed | tf_op | source)
XLA Modules:
  0.0 441.5 jit_solution(9110982626781433239)
XLA Ops:
  1.3 3.3 collective-permute-start.1
  4.7 3.5 collective-permute-start
  8.2 5.4 %slice_convert_fusion = (f32[1,2,128,2048]{3,2,1,0:T(8,128)S(1)}, f32[1,2,128,2048]{3,2,1,0:T(8,128)}, f32[1,2,128,2048]{3,2,1,0:T(8,128)}, f32[1,2,128,2048]{3,2,1,0:T(8,128)}) fusion(bf16[1,2,512,2048]{3,2,1,0:T(8,128)(2,1)} %param.19), kind=kLoop, calls=%fused_computation.123 | loop fusion | flops 2097152 | bytes 12582912 | tf_op jit(solution)/shard_map/convert_element_type | solution.py:79
  18.8 2.4 copy.6
  21.3 5.0 %fusion.35 = (f32[2,393088]{1,0:T(2,128)}, f32[2,393088]{1,0:T(2,128)}, f32[2,393088]{1,0:T(2,128)}, f32[2,393088]{1,0:T(2,128)}) fusion(f32[2,393216]{1,0:T(2,128)S(1)} %bitcast.460), kind=kLoop, calls=%fused_computation.182 | loop fusion | bytes 18869248 | tf_op jit(solution)/shard_map/slice | solution.py:42
  26.2 5.0 %pad_slice_fusion = (f32[2,393344]{1,0:T(2,128)}, f32[2,393344]{1,0:T(2,128)}, f32[2,393344]{1,0:T(2,128)}, f32[2,393344]{1,0:T(2,128)}) fusion(f32[2,393216]{1,0:T(2,128)S(1)} %bitcast.461), kind=kLoop, calls=%fused_computation | loop fusion | bytes 15732736 | tf_op jit(solution)/shard_map/slice | solution.py:42
  31.2 6.8 %reshape.906 = f32[2,128,3071]{2,1,0:T(8,128)} reshape(f32[2,393088]{1,0:T(2,128)} %get-tuple-element.164) | data formatting | bytes 6289408 | tf_op jit(solution)/shard_map/reshape | solution.py:43
  38.0 6.7 %reshape.910 = f32[2,128,3071]{2,1,0:T(8,128)} reshape(f32[2,393088]{1,0:T(2,128)} %get-tuple-element.163) | data formatting | bytes 6289408 | tf_op jit(solution)/shard_map/reshape | solution.py:43
  44.7 7.9 %reshape.909 = f32[2,128,3073]{2,1,0:T(8,128)} reshape(f32[2,393344]{1,0:T(2,128)} %get-tuple-element.167) | data formatting | bytes 6293504 | tf_op jit(solution)/shard_map/reshape | solution.py:43
  52.7 8.4 %reshape.905 = f32[2,128,3073]{2,1,0:T(8,128)} reshape(f32[2,393344]{1,0:T(2,128)} %get-tuple-element.168) | data formatting | bytes 6293504 | tf_op jit(solution)/shard_map/reshape | solution.py:43
  61.0 7.4 %add_reduce_fusion.2 = (f32[]{:T(128)}, f32[128]{0:T(128)S(1)}, f32[128]{0:T(128)S(1)}, f32[1,128,2048]{2,1,0:T(8,128)}, f32[1,128,2048]{2,1,0:T(8,128)}, /*inde...) fusion(f32[128]{0:T(128)S(1)} %get-tuple-element.174, ...), kind=kLoop, calls=%fused_computation.99 | loop fusion | flops 13630974 | bytes 16781320 | tf_op jit(solution)/shard_map/reduce_sum | solution.py:82
  69.0 2.5 multiply_add_fusion.17
  72.0 1.5 pad_maximum_fusion
  73.5 16.7 %rev.12 = f32[2,128,2048]{2,1,0:T(8,128)} reverse(f32[2,128,2048]{2,1,0:T(8,128)} %pad_maximum_fusion), dimensions={1} | reverse | bytes 4194304 | tf_op jit(solution)/shard_map/rev | solution.py:101
  90.2 1.8 pad_bitcast_fusion.3
  91.9 1.7 copy.11
  93.7 1.9 slice.544
  95.6 5.9 %reshape.922 = f32[2,128,2175]{2,1,0:T(8,128)} reshape(f32[2,278400]{1,0:T(2,128)} %slice.544) | data formatting | bytes 4454400 | tf_op jit(solution)/shard_map/reshape | solution.py:43
  101.5 1.8 reduce_sum.202
  103.3 6.1 %multiply_add_fusion.14 = (f32[1,128,2048]{2,1,0:T(8,128)}, f32[1,128,2048]{2,1,0:T(8,128)S(1)}, f32[1,128,2048]{2,1,0:T(8,128)S(1)}, f32[1,128,2048]{2,1,0:T(8,...) fusion(f32[128]{0:T(128)S(1)} %get-tuple-element.174, f32[128]{0:T(128)S(1)} %get-tuple-element.175, ...), kind=kLoop, calls=%fused_computation.132 | loop fusion | flops 6815744 | bytes 14681088 | tf_op jit(solution)/shard_map/add | solution.py:88
  109.5 1.5 multiply_subtract_fusion.14
  111.0 1.6 pad_maximum_fusion.1
  112.6 16.7 %rev.13 = f32[2,128,2048]{2,1,0:T(8,128)} reverse(f32[2,128,2048]{2,1,0:T(8,128)} %pad_maximum_fusion.1), dimensions={1} | reverse | bytes 4194304 | tf_op jit(solution)/shard_map/rev | solution.py:101
  129.3 1.8 pad_bitcast_fusion.2
  131.0 1.7 copy.12
  132.8 2.0 slice.545
  134.8 5.9 %reshape.924 = f32[2,128,2175]{2,1,0:T(8,128)} reshape(f32[2,278400]{1,0:T(2,128)} %slice.545) | data formatting | bytes 4454400 | tf_op jit(solution)/shard_map/reshape | solution.py:43
  140.7 1.8 reduce_sum.203
  142.5 6.7 %reshape.914 = f32[2,128,3071]{2,1,0:T(8,128)} reshape(f32[2,393088]{1,0:T(2,128)} %get-tuple-element.162) | data formatting | bytes 6289408 | tf_op jit(solution)/shard_map/reshape | solution.py:43
  149.2 6.7 %reshape.918 = f32[2,128,3071]{2,1,0:T(8,128)} reshape(f32[2,393088]{1,0:T(2,128)} %get-tuple-element.161) | data formatting | bytes 6289408 | tf_op jit(solution)/shard_map/reshape | solution.py:43
  155.9 8.1 %reshape.917 = f32[2,128,3073]{2,1,0:T(8,128)} reshape(f32[2,393344]{1,0:T(2,128)} %get-tuple-element.165) | data formatting | bytes 6293504 | tf_op jit(solution)/shard_map/reshape | solution.py:43
  164.1 8.0 %reshape.913 = f32[2,128,3073]{2,1,0:T(8,128)} reshape(f32[2,393344]{1,0:T(2,128)} %get-tuple-element.166) | data formatting | bytes 6293504 | tf_op jit(solution)/shard_map/reshape | solution.py:43
  172.0 6.9 %add_reduce_fusion = (f32[]{:T(128)}, f32[128]{0:T(128)S(1)}, f32[128]{0:T(128)S(1)}, f32[1,128,2048]{2,1,0:T(8,128)}, f32[1,128,2048]{2,1,0:T(8,128)}, /*index=...) fusion(f32[128]{0:T(128)S(1)} %get-tuple-element.178, ...), kind=kLoop, calls=%fused_computation.97 | loop fusion | flops 13630974 | bytes 16781320 | tf_op jit(solution)/shard_map/reduce_sum | solution.py:82
  179.4 2.5 multiply_add_fusion.11
  183.4 1.6 pad_maximum_fusion.2
  185.0 16.7 %rev.14 = f32[2,128,2048]{2,1,0:T(8,128)} reverse(f32[2,128,2048]{2,1,0:T(8,128)} %pad_maximum_fusion.2), dimensions={1} | reverse | bytes 4194304 | tf_op jit(solution)/shard_map/rev | solution.py:101
  201.6 1.8 pad_bitcast_fusion.1
  203.4 1.7 copy.13
  205.1 2.3 slice.547
  207.4 6.0 %reshape.926 = f32[2,128,2175]{2,1,0:T(8,128)} reshape(f32[2,278400]{1,0:T(2,128)} %slice.547) | data formatting | bytes 4454400 | tf_op jit(solution)/shard_map/reshape | solution.py:43
  213.3 1.8 reduce_sum.204
  215.1 5.3 %multiply_add_fusion.8 = (f32[1,128,2048]{2,1,0:T(8,128)}, f32[1,128,2048]{2,1,0:T(8,128)S(1)}, f32[1,128,2048]{2,1,0:T(8,128)S(1)}, f32[1,128,2048]{2,1,0:T(8,1...) fusion(f32[128]{0:T(128)S(1)} %get-tuple-element.178, f32[128]{0:T(128)S(1)} %get-tuple-element.171, ...), kind=kLoop, calls=%fused_computation.118 | loop fusion | flops 6815744 | bytes 14681088 | tf_op jit(solution)/shard_map/add | solution.py:88
  222.1 10.5 %rev.15 = f32[2,128,2048]{2,1,0:T(8,128)} reverse(f32[2,128,2048]{2,1,0:T(8,128)S(1)} %pad_maximum_fusion.3), dimensions={1} | reverse | bytes 4194304 | tf_op jit(solution)/shard_map/rev | solution.py:101
  232.6 1.8 pad_bitcast_fusion
  234.4 1.7 copy.14
  236.1 2.0 slice.549
  238.1 4.6 %reshape.928 = f32[2,128,2175]{2,1,0:T(8,128)S(1)} reshape(f32[2,278400]{1,0:T(2,128)} %slice.549) | data formatting | bytes 4454400 | tf_op jit(solution)/shard_map/reshape | solution.py:43
  244.2 1.7 copy.7
  245.9 1.9 slice.518
  247.8 4.6 %reshape.908 = f32[2,128,2175]{2,1,0:T(8,128)S(1)} reshape(f32[2,278400]{1,0:T(2,128)} %slice.518) | data formatting | bytes 4454400 | tf_op jit(solution)/shard_map/reshape | solution.py:43
  255.0 1.7 copy.8
  256.7 2.1 slice.525
  258.8 4.6 %reshape.912 = f32[2,128,2175]{2,1,0:T(8,128)S(1)} reshape(f32[2,278400]{1,0:T(2,128)} %slice.525) | data formatting | bytes 4454400 | tf_op jit(solution)/shard_map/reshape | solution.py:43
  266.0 1.7 copy.9
  267.7 1.9 slice.533
  269.6 4.6 %reshape.916 = f32[2,128,2175]{2,1,0:T(8,128)S(1)} reshape(f32[2,278400]{1,0:T(2,128)} %slice.533) | data formatting | bytes 4454400 | tf_op jit(solution)/shard_map/reshape | solution.py:43
  276.7 1.7 copy.10
  278.5 2.1 slice.542
  280.6 4.6 %reshape.920 = f32[2,128,2175]{2,1,0:T(8,128)S(1)} reshape(f32[2,278400]{1,0:T(2,128)} %slice.542) | data formatting | bytes 4454400 | tf_op jit(solution)/shard_map/reshape | solution.py:43
  289.0 1.9 collective-permute-start.3
  293.9 3.6 collective-permute-start.2
  300.1 67.9 %all-reduce.19 = (f32[2,512]{1,0:T(2,128)S(1)}, f32[]{:T(128)}) all-reduce(f32[2,512]{1,0:T(2,128)S(1)} %pad_maximum_fusion.5, f32[]{:T(128)S(6)} %add.347), channel_id=1, replica_groups=mesh['chan'=16,'sub'=8] {'chan','sub'}, use_global_device_ids=true, to_apply=%region_26.27 | all-reduce | flops 1025 | bytes 8200 | tf_op jit(solution)/shard_map/psum | solution.py:112
  370.0 32.4 %psum.28 = f32[2,2048]{1,0:T(2,128)S(1)} all-reduce(f32[2,2048]{1,0:T(2,128)S(1)} %fusion.34), channel_id=1, replica_groups=mesh['chan'=16,'sub'=8] {'sub'}, use_global_device_ids=true, to_apply=%region_15.16 | all-reduce | flops 4096 | bytes 32768 | tf_op jit(solution)/shard_map/psum | solution.py:111
  403.6 35.2 %psum.29 = f32[]{:T(128)} all-reduce(f32[]{:T(128)} %multiply_reduce_fusion), channel_id=1, replica_groups=mesh['chan'=16,'sub'=8] {'chan'}, use_global_device_ids=true, to_apply=%region_17.18 | all-reduce | flops 1 | bytes 8 | tf_op jit(solution)/shard_map/psum | solution.py:113
  (77 shorter events, 29.0 us)
Async XLA Ops:
  1.3 17.1 %collective-permute-start.1 = (f32[2,512]{1,0:T(2,128)S(1)}, f32[2,512]{1,0:T(2,128)S(1)}, u32[]{:S(2)}, u32[]{:S(2)}) collective-permute-start(f32[2,512]{1,0:T(2,128)S(1)} %get-tuple-element.170), channel_id=1, source_target_pairs={{8,0},{16,8},{24,16},{32,24},{40,32},{48,40},{56,48},{64,56},{72,6... | collective-permute-start | bytes 12296 | tf_op jit(solution)/shard_map/ppermute | solution.py:22
  4.7 9.0 %copy-start.10 = (f32[2,512]{1,0:T(2,128)S(1)}, f32[2,512]{1,0:T(2,128)}, u32[]{:S(2)}) copy-start(f32[2,512]{1,0:T(2,128)} %param.21) | copy-start | bytes 12292
  4.7 13.8 %copy-start.9 = (f32[2,2048]{1,0:T(2,128)S(1)}, f32[2,2048]{1,0:T(2,128)}, u32[]{:S(2)}) copy-start(f32[2,2048]{1,0:T(2,128)} %param.20) | copy-start | bytes 49156
  4.7 13.8 %collective-permute-start = (f32[2,512]{1,0:T(2,128)S(1)}, f32[2,512]{1,0:T(2,128)S(1)}, u32[]{:S(2)}, u32[]{:S(2)}) collective-permute-start(f32[2,512]{1,0:T(2,128)S(1)} %get-tuple-element.169), channel_id=1, source_target_pairs={{0,8},{8,16},{16,24},{24,32},{32,40},{40,48},{48,56},{56,64},{64,7... | collective-permute-start | bytes 12296 | tf_op jit(solution)/shard_map/ppermute | solution.py:19
  61.0 7.4 %copy-start.1 = (f32[1,2,128,2048]{3,2,1,0:T(8,128)S(1)}, f32[1,2,128,2048]{3,2,1,0:T(8,128)}, u32[]{:S(2)}) copy-start(f32[1,2,128,2048]{3,2,1,0:T(8,128)} %get-tuple-element.159) | copy-start | bytes 6291460
  61.0 7.4 %copy-start.3 = (f32[2,128,3071]{2,1,0:T(8,128)S(1)}, f32[2,128,3071]{2,1,0:T(8,128)}, u32[]{:S(2)}) copy-start(f32[2,128,3071]{2,1,0:T(8,128)} %reshape.906) | copy-start | bytes 9434116
  61.0 7.9 %copy-start.5 = (f32[2,128,3073]{2,1,0:T(8,128)S(1)}, f32[2,128,3073]{2,1,0:T(8,128)}, u32[]{:S(2)}) copy-start(f32[2,128,3073]{2,1,0:T(8,128)} %reshape.905) | copy-start | bytes 9440260
  172.0 6.9 %copy-start = (f32[1,2,128,2048]{3,2,1,0:T(8,128)S(1)}, f32[1,2,128,2048]{3,2,1,0:T(8,128)}, u32[]{:S(2)}) copy-start(f32[1,2,128,2048]{3,2,1,0:T(8,128)} %get-tuple-element.160) | copy-start | bytes 6291460
  172.0 6.9 %copy-start.2 = (f32[2,128,3071]{2,1,0:T(8,128)S(1)}, f32[2,128,3071]{2,1,0:T(8,128)}, u32[]{:S(2)}) copy-start(f32[2,128,3071]{2,1,0:T(8,128)} %reshape.914) | copy-start | bytes 9434116
  172.0 7.3 %copy-start.4 = (f32[2,128,3073]{2,1,0:T(8,128)S(1)}, f32[2,128,3073]{2,1,0:T(8,128)}, u32[]{:S(2)}) copy-start(f32[2,128,3073]{2,1,0:T(8,128)} %reshape.913) | copy-start | bytes 9440260
  252.4 1.2 copy-start.6
  263.4 1.2 copy-start.7
  274.1 1.2 copy-start.8
  289.0 81.0 %collective-permute-start.3 = (f32[2,512]{1,0:T(2,128)S(1)}, f32[2,512]{1,0:T(2,128)S(1)}, u32[]{:S(2)}, u32[]{:S(2)}) collective-permute-start(f32[2,512]{1,0:T(2,128)S(1)} %slice.552), channel_id=1, source_target_pairs={{8,0},{16,8},{24,16},{32,24},{40,32},{48,40},{56,48},{64,56},{72,6... | collective-permute-start | bytes 12296 | tf_op jit(solution)/shard_map/ppermute | solution.py:30
  293.9 76.1 %collective-permute-start.2 = (f32[2,512]{1,0:T(2,128)S(1)}, f32[2,512]{1,0:T(2,128)S(1)}, u32[]{:S(2)}, u32[]{:S(2)}) collective-permute-start(f32[2,512]{1,0:T(2,128)S(1)} %slice.551), channel_id=1, source_target_pairs={{0,8},{8,16},{16,24},{24,32},{32,40},{40,48},{48,56},{56,64},{64,7... | collective-permute-start | bytes 12296 | tf_op jit(solution)/shard_map/ppermute | solution.py:30
where the time goes:
time: 450 us; the launch traced here: 442 us
  local copies, waits for them, and re-layouts  217 us (48%)
  blocking collectives  135 us (30%)
  other arithmetic  69.5 us (15%)
  starting transfers between devices  12.4 us (3%)
  between operations  7.12 us (2%)
    reshape x16, local copies, waits for them, and re-layouts, shifted_rows(): return flattened.reshape(leading + (row_count, row_span))[..., :length]  99.9 us
    psum x1, blocking collectives, on_device(): lax.psum((profile_local, error_sum), ('chan', 'sub'))  67.9 us
    rev x4, local copies, waits for them, and re-layouts, on_device(): lower_term[:, ::-1]  60.5 us
    psum x1, blocking collectives, on_device(): squares = lax.psum(jnp.sum(filter_grad * filter_grad), 'chan')  35.2 us
    psum x1, blocking collectives, on_device(): filter_grad = lax.psum(filter_local, 'sub')  32.4 us
    unnamed x36, local copies, waits for them, and re-layouts  27.1 us
    slice x10, local copies, waits for them, and re-layouts, shifted_rows(): lax.slice_in_dim(flattened, start, start + row_count * row_span, axis=len...  26.2 us
    add x4, other arithmetic, on_device(): left_re * prof_re + left_im * prof_im  16.6 us
  transfers between devices with their start and end apart: 4, of which 0 were waited for; matrix products, arithmetic and copies ran while one was open for 3% of the time, Pallas kernels for 0%

commit v1 on v0

v1 whole, which is shorter than its diff:
```python
import functools

import jax
import jax.numpy as jnp
from jax import lax
from jax.experimental import pallas as pl
from jax.experimental.pallas import tpu as pltpu
from jax.sharding import PartitionSpec as P

CHANNELS = 32768
LANES = 128
ROWS = 128
GROUP = 16

filter_rate = 0.1
profile_rate = 0.1
epsilon = 1e-06


def skew(block, sign):
    width = block.shape[1]
    row = lax.broadcasted_iota(jnp.int32, block.shape, 0)
    for bit in (1, 2, 4):
        moved = pltpu.roll(block, bit if sign > 0 else width - bit, 1)
        block = jnp.where((row & bit) != 0, moved, block)
    return block


def gradient_kernel(
    factor, spectra, low, own, high, prof, out,
    fwd_re, fwd_im, bwd_re, bwd_im, up_re, up_im, down_re, down_im, part_re, part_im, err
):
    step = pl.program_id(0)
    owned = own.shape[1]
    halo = low.shape[1]
    width = owned + 2 * halo
    harmonics = prof.shape[0]
    chan = lax.axis_index("chan")
    last = lax.axis_size("chan") - 1

    @pl.when(step == 0)
    def _():
        keep_low = jnp.where(chan == 0, 0.0, 1.0).astype(jnp.float32)
        keep_high = jnp.where(chan == last, 0.0, 1.0).astype(jnp.float32)
        for part, fwd, bwd in ((0, fwd_re, bwd_re), (1, fwd_im, bwd_im)):
            line = jnp.concatenate(
                [
                    low[part : part + 1, :] * keep_low,
                    own[part : part + 1, :],
                    high[part : part + 1, :] * keep_high,
                ],
                axis=1,
            )
            base = jnp.broadcast_to(line, (8, width))
            right = skew(base, 1)
            left = skew(base, -1)
            for a in range(ROWS // 8):
                rows = pl.ds(8 * a, 8)
                bwd[rows, :] = pltpu.roll(right, 8 * a, 1) if a else right
                fwd[rows, :] = pltpu.roll(left, width - 8 * a, 1) if a else left
        for acc in (up_re, up_im, down_re, down_im):
            acc[...] = jnp.zeros_like(acc)
        err[...] = jnp.zeros_like(err)

    shift = step * ROWS

    def group(index, carry):
        start = pl.multiple_of(index * GROUP, GROUP)
        rows = pl.ds(start, GROUP)
        krows = pl.ds(pl.multiple_of(shift + start, GROUP), GROUP)
        q_re = jnp.broadcast_to(prof[krows, 0:1], (GROUP, LANES))
        q_im = jnp.broadcast_to(prof[krows, 1:2], (GROUP, LANES))
        a_re = jnp.zeros((GROUP, LANES), jnp.float32)
        a_im = jnp.zeros((GROUP, LANES), jnp.float32)
        e_sum = jnp.zeros((GROUP, LANES), jnp.float32)
        for tile in range(owned // LANES):
            cols = pl.ds(tile * LANES, LANES)
            above = pl.ds(pl.multiple_of(halo + tile * LANES + shift, LANES), LANES)
            below = pl.ds(pl.multiple_of(halo + tile * LANES - shift, LANES), LANES)
            s_re = spectra[0, 0, rows, cols].astype(jnp.float32)
            s_im = spectra[0, 1, rows, cols].astype(jnp.float32)
            f_re = fwd_re[rows, above]
            f_im = fwd_im[rows, above]
            b_re = bwd_re[rows, below]
            b_im = bwd_im[rows, below]
            p_re = f_re * b_re + f_im * b_im
            p_im = f_im * b_re - f_re * b_im
            r_re = s_re - (p_re * q_re - p_im * q_im)
            r_im = s_im - (p_re * q_im + p_im * q_re)
            e_sum = e_sum + (r_re * r_re + r_im * r_im)
            a_re = a_re + (r_re * p_re + r_im * p_im)
            a_im = a_im + (r_im * p_re - r_re * p_im)
            x_re = r_re * q_re + r_im * q_im
            x_im = r_im * q_re - r_re * q_im
            up_re[rows, above] += x_re * b_re - x_im * b_im
            up_im[rows, above] += x_re * b_im + x_im * b_re
            down_re[rows, below] += x_re * f_re + x_im * f_im
            down_im[rows, below] += x_re * f_im - x_im * f_re
        part_re[krows, :] = a_re
        part_im[krows, :] = a_im
        err[...] += e_sum
        return carry

    lax.fori_loop(0, ROWS // GROUP, group, 0)

    @pl.when(step == pl.num_programs(0) - 1)
    def _():
        ones = jnp.ones((8, LANES), jnp.float32)
        for part, up, down, sums in (
            (0, up_re, down_re, part_re),
            (1, up_im, down_im, part_im),
        ):
            total_up = up[0:8, :]
            total_down = down[0:8, :]
            for a in range(1, ROWS // 8):
                rows = pl.ds(8 * a, 8)
                total_up = total_up + pltpu.roll(up[rows, :], 8 * a, 1)
                total_down = total_down + pltpu.roll(down[rows, :], width - 8 * a, 1)
            total = skew(total_up, 1) + skew(total_down, -1)
            line = factor * jnp.sum(total, axis=0, keepdims=True)
            out[part : part + 1, 0:width] = line
            reduced = lax.dot_general(
                ones,
                sums[...],
                (((1,), (1,)), ((), ())),
                precision=lax.Precision.HIGHEST,
                preferred_element_type=jnp.float32,
            )
            out[part : part + 1, width : width + harmonics] = factor * reduced[0:1, :]
        out[0:1, width + harmonics :] = jnp.sum(err[...], axis=0, keepdims=True)
        out[1:2, width + harmonics :] = jnp.zeros((1, LANES), jnp.float32)


def local_gradients(factor, spectra, low, own, high, prof):
    harmonics = prof.shape[0]
    halo = low.shape[1]
    owned = own.shape[1]
    width = owned + 2 * halo
    table = pltpu.VMEM((ROWS, width), jnp.float32)
    whole = lambda shape: pl.BlockSpec(shape, lambda i: (0, 0))
    return pl.pallas_call(
        functools.partial(gradient_kernel, factor),
        grid=(harmonics // ROWS,),
        in_specs=[
            pl.BlockSpec((1, 2, ROWS, owned), lambda i: (0, 0, i, 0)),
            whole(low.shape),
            whole(own.shape),
            whole(high.shape),
            whole(prof.shape),
        ],
        out_specs=whole((2, width + harmonics + LANES)),
        out_shape=jax.ShapeDtypeStruct((2, width + harmonics + LANES), jnp.float32),
        scratch_shapes=[table] * 8
        + [pltpu.VMEM((harmonics, LANES), jnp.float32)] * 2
        + [pltpu.VMEM((GROUP, LANES), jnp.float32)],
        compiler_params=pltpu.CompilerParams(vmem_limit_bytes=40 * 1024 * 1024),
    )(spectra, low, own, high, prof)


def neighbours(to_next, to_previous, axis):
    count = lax.axis_size(axis)
    ahead = [(i, (i + 1) % count) for i in range(count)]
    back = [(target, source) for source, target in ahead]
    return lax.ppermute(to_next, axis, ahead), lax.ppermute(to_previous, axis, back)


def sum_over(values, axis, masks):
    count = lax.axis_size(axis)
    for mask in masks:
        values = values + lax.ppermute(values, axis, [(i, i ^ mask) for i in range(count)])
    return values


def on_device(spectra, filter_init, profile_init):
    harmonics = profile_init.shape[1]
    owned = filter_init.shape[1]
    weight = 1.0 / (lax.axis_size("sub") * spectra.shape[0] * harmonics)
    chan = lax.axis_index("chan")
    low, high = neighbours(filter_init[:, owned - harmonics :], filter_init[:, :harmonics], "chan")
    sums = local_gradients(-2.0 * weight, spectra, low, filter_init, high, profile_init.T)
    from_below, from_above = neighbours(
        sums[:, harmonics + owned : 2 * harmonics + owned], sums[:, :harmonics], "chan"
    )
    from_below = jnp.where(chan == 0, 0.0, from_below)
    from_above = jnp.where(chan == lax.axis_size("chan") - 1, 0.0, from_above)
    local = sums[:, harmonics : harmonics + owned]
    local = jnp.concatenate(
        [
            local[:, :harmonics] + from_below,
            local[:, harmonics : owned - harmonics],
            local[:, owned - harmonics :] + from_above,
            sums[:, owned + 2 * harmonics :],
        ],
        axis=1,
    )
    local = sum_over(local, "sub", (2, 6, 1))
    filter_grad = local[:, :owned]
    squares = jnp.sum(filter_grad * filter_grad)
    rest = local[:, owned:]
    rest = rest.at[1, harmonics].set(squares)
    rest = sum_over(rest, "chan", (1, 2, 4, 12))
    profile_grad = rest[:, :harmonics]
    error_total = jnp.sum(rest[0, harmonics:])
    squares = rest[1, harmonics]
    filter_out = filter_init - filter_rate * filter_grad / jnp.sqrt(
        squares / (2 * CHANNELS) + epsilon
    )
    profile_out = profile_init - profile_rate * profile_grad / jnp.sqrt(
        jnp.mean(profile_grad * profile_grad) + epsilon
    )
    return (filter_out, profile_out, (error_total * weight / CHANNELS)[None])


def solution(mesh):
    return jax.shard_map(
        on_device,
        mesh=mesh,
        in_specs=(P("sub", None, None, "chan"), P(None, "chan"), P()),
        out_specs=(P(None, "chan"), P(), P()),
        check_vma=False,
    )
```

time: 450 us -> 66.8 us (0.15)
  the two profiles are of different devices: /device:TPU:1 before, /device:TPU:0 now
where the time goes in v1:
time: 66.8 us; the launch traced here: 66.4 us
  waiting for transfers between devices  25.7 us (38%)
  Pallas kernels  14.6 us (22%)
  starting transfers between devices  13.2 us (20%)
  local copies, waits for them, and re-layouts  5.7 us (9%)
  between operations  3.97 us (6%)
  other arithmetic  3.19 us (5%)
    ppermute x7, waiting for transfers between devices, sum_over(): lax.ppermute(values, axis, [(i, i ^ mask) for i in range(count)])  18.8 us
    pallas_call x1, Pallas kernels, local_gradients(): pl.pallas_call(functools.partial(gradient_kernel, factor), grid=(harmonic...  14.6 us
    ppermute x7, starting transfers between devices, sum_over(): lax.ppermute(values, axis, [(i, i ^ mask) for i in range(count)])  9.18 us
    ppermute x2, waiting for transfers between devices, neighbours(): lax.ppermute(to_next, axis, ahead)  5.52 us
    ppermute x2, starting transfers between devices, neighbours(): lax.ppermute(to_previous, axis, back)  3.89 us
    unnamed x9, local copies, waits for them, and re-layouts  3.74 us
    ppermute x2, waiting for transfers between devices, neighbours(): lax.ppermute(to_previous, axis, back)  1.34 us
  transfers between devices with their start and end apart: 11, of which 10 were waited for; matrix products, arithmetic and copies ran while one was open for 1% of the time, Pallas kernels for 0%

profile of v1, /device:TPU:0, one launch (start us, length us, event | category | flops | bytes accessed | tf_op | source)
XLA Modules:
  0.0 66.4 jit_solution(7905757967647012863)
XLA Ops:
  0.6 0.0 copy-start.2
  0.6 0.0 copy-start.3
  0.7 0.7 %fusion = (f32[2,512]{1,0:T(2,128)S(1)}, f32[2,512]{1,0:T(2,128)S(1)}) fusion(f32[2,2048]{1,0:T(2,128)} %own.1), kind=kLoop, calls=%fused_computation.8 | loop fusion | bytes 16384 | tf_op jit(solution)/shard_map/slice | solution.py:179
  1.4 0.0 collective-permute-start
  1.4 3.9 %collective-permute-start.1 = (f32[2,512]{1,0:T(2,128)S(1)}, f32[2,512]{1,0:T(2,128)S(1)}, u32[]{:S(2)}, u32[]{:S(2)}) collective-permute-start(f32[2,512]{1,0:T(2,128)S(1)} %get-tuple-element.17), channel_id=1, source_target_pairs={{8,0},{16,8},{24,16},{32,24},{40,32},{48,40},{56,48},{64,56},{72,6... | collective-permute-start | bytes 12296 | tf_op jit(solution)/shard_map/ppermute | solution.py:164
  5.3 0.8 %copy.6 = f32[2,512]{0,1:T(8,128)S(1)} copy(f32[2,512]{1,0:T(2,128)} %param.7) | data formatting | bytes 8192 | tf_op args[2]
  6.1 0.5 collective-permute-done.low
  6.6 0.0 collective-permute-done.1.high
  6.6 0.0 copy-start
  6.6 2.2 %copy-done = bf16[1,2,512,2048]{3,2,1,0:T(8,128)(2,1)S(1)} copy-done((bf16[1,2,512,2048]{3,2,1,0:T(8,128)(2,1)S(1)}, bf16[1,2,512,2048]{3,2,1,0:T(8,128)(2,1)}, u32[]{:S(2)}) %copy-start) | copy-done | bytes 4194328
  8.8 0.0 copy-start.1
  8.8 0.7 %copy-done.1 = f32[2,2048]{1,0:T(2,128)S(1)} copy-done((f32[2,2048]{1,0:T(2,128)S(1)}, f32[2,2048]{1,0:T(2,128)}, u32[]{:S(2)}) %copy-start.1) | copy-done | bytes 16408
  9.5 14.6 %shard_map.58 = f32[2,3712]{1,0:T(2,128)S(1)} custom-call(bf16[1,2,512,2048]{3,2,1,0:T(8,128)(2,1)S(1)} %copy-done, f32[2,512]{1,0:T(2,128)S(1)} %collective-permute-done.low, f32[2,2048]{1,0:T(2,128)S(1)} %copy-done.1, f32[2,512]{1,0:T(2,128)S(1)} %collective-permute-done.1.high, f32[512,2]{1,0:T(8,128)S(1)} %bitcast.4), custom_call_target="tpu_custom_call" | custom-call | tf_op jit(solution)/shard_map/pallas_call | solution.py:141
  24.2 0.1 collective-permute-start.2
  24.3 5.1 %collective-permute-done.2 = f32[2,512]{1,0:T(2,128)S(1)} collective-permute-done((f32[2,512]{1,0:T(2,128)S(1)}, f32[2,512]{1,0:T(2,128)S(1)}, u32[]{:S(2)}, u32[]{:S(2)}) %collective-permute-start.2) | collective-permute-done | bytes 4128 | tf_op jit(solution)/shard_map/ppermute | solution.py:164
  29.4 0.0 collective-permute-start.3
  29.4 1.3 %collective-permute-done.3 = f32[2,512]{1,0:T(2,128)S(1)} collective-permute-done((f32[2,512]{1,0:T(2,128)S(1)}, f32[2,512]{1,0:T(2,128)S(1)}, u32[]{:S(2)}, u32[]{:S(2)}) %collective-permute-start.3) | collective-permute-done | bytes 4128 | tf_op jit(solution)/shard_map/ppermute | solution.py:164
  30.7 1.6 %collective-permute-start.4 = (f32[2,2688]{1,0:T(2,128)S(1)}, f32[2,2688]{1,0:T(2,128)S(1)}, u32[]{:S(2)}, u32[]{:S(2)}) collective-permute-start(f32[2,2688]{1,0:T(2,128)S(1)} %pad_maximum_fusion), channel_id=1, source_target_pairs={{0,2},{1,3},{2,0},{3,1},{4,6},{5,7},{6,4},{7,5},{8,10},{9,11},{10,... | collective-permute-start | bytes 64520 | tf_op jit(solution)/shard_map/ppermute | solution.py:170
  32.4 2.3 %collective-permute-done.4 = f32[2,2688]{1,0:T(2,128)S(1)} collective-permute-done((f32[2,2688]{1,0:T(2,128)S(1)}, f32[2,2688]{1,0:T(2,128)S(1)}, u32[]{:S(2)}, u32[]{:S(2)}) %collective-permute-start.4) | collective-permute-done | bytes 21536 | tf_op jit(solution)/shard_map/ppermute | solution.py:170
  34.6 2.9 %collective-permute-start.5 = (f32[2,2688]{1,0:T(2,128)S(1)}, f32[2,2688]{1,0:T(2,128)S(1)}, u32[]{:S(2)}, u32[]{:S(2)}) collective-permute-start(f32[2,2688]{1,0:T(2,128)S(1)} %fusion.1), channel_id=1, source_target_pairs={{0,6},{1,7},{2,4},{3,5},{4,2},{5,3},{6,0},{7,1},{8,14},{9,15},{10,... | collective-permute-start | bytes 64520 | tf_op jit(solution)/shard_map/ppermute | solution.py:170
  37.5 2.2 %collective-permute-done.5 = f32[2,2688]{1,0:T(2,128)S(1)} collective-permute-done((f32[2,2688]{1,0:T(2,128)S(1)}, f32[2,2688]{1,0:T(2,128)S(1)}, u32[]{:S(2)}, u32[]{:S(2)}) %collective-permute-start.5) | collective-permute-done | bytes 21536 | tf_op jit(solution)/shard_map/ppermute | solution.py:170
  39.7 4.0 %collective-permute-start.6 = (f32[2,2688]{1,0:T(2,128)S(1)}, f32[2,2688]{1,0:T(2,128)S(1)}, u32[]{:S(2)}, u32[]{:S(2)}) collective-permute-start(f32[2,2688]{1,0:T(2,128)S(1)} %add.39), channel_id=1, source_target_pairs={{0,1},{1,0},{2,3},{3,2},{4,5},{5,4},{6,7},{7,6},{8,9},{9,8},{10,11... | collective-permute-start | bytes 64520 | tf_op jit(solution)/shard_map/ppermute | solution.py:170
  43.7 1.8 %collective-permute-done.6 = f32[2,2688]{1,0:T(2,128)S(1)} collective-permute-done((f32[2,2688]{1,0:T(2,128)S(1)}, f32[2,2688]{1,0:T(2,128)S(1)}, u32[]{:S(2)}, u32[]{:S(2)}) %collective-permute-start.6) | collective-permute-done | bytes 21536 | tf_op jit(solution)/shard_map/ppermute | solution.py:170
  45.5 0.6 multiply_reduce_fusion
  46.2 0.7 %scatter.4 = f32[2,640]{1,0:T(2,128)S(1)} dynamic-update-slice(f32[2,640]{1,0:T(2,128)S(1)} %slice.82, f32[1,1]{1,0:T(1,128)} %bitcast.1, s32[]{:T(128)} %constant.54.clone.1, s32[]{:T(128)} %constant.55.clone.1) | dynamic-update-slice | bytes 12 | tf_op jit(solution)/shard_map/scatter | solution.py:200
  46.9 0.1 collective-permute-start.7
  47.0 1.2 %collective-permute-done.7 = f32[2,640]{1,0:T(2,128)S(1)} collective-permute-done((f32[2,640]{1,0:T(2,128)S(1)}, f32[2,640]{1,0:T(2,128)S(1)}, u32[]{:S(2)}, u32[]{:S(2)}) %collective-permute-start.7) | collective-permute-done | bytes 5152 | tf_op jit(solution)/shard_map/ppermute | solution.py:170
  48.1 0.0 collective-permute-start.8
  48.1 3.6 %collective-permute-done.8 = f32[2,640]{1,0:T(2,128)S(1)} collective-permute-done((f32[2,640]{1,0:T(2,128)S(1)}, f32[2,640]{1,0:T(2,128)S(1)}, u32[]{:S(2)}, u32[]{:S(2)}) %collective-permute-start.8) | collective-permute-done | bytes 5152 | tf_op jit(solution)/shard_map/ppermute | solution.py:170
  51.7 0.0 collective-permute-start.9
  51.7 3.6 %collective-permute-done.9 = f32[2,640]{1,0:T(2,128)S(1)} collective-permute-done((f32[2,640]{1,0:T(2,128)S(1)}, f32[2,640]{1,0:T(2,128)S(1)}, u32[]{:S(2)}, u32[]{:S(2)}) %collective-permute-start.9) | collective-permute-done | bytes 5152 | tf_op jit(solution)/shard_map/ppermute | solution.py:170
  55.4 0.6 collective-permute-start.10
  56.0 4.2 %collective-permute-done.10 = f32[2,640]{1,0:T(2,128)S(1)} collective-permute-done((f32[2,640]{1,0:T(2,128)S(1)}, f32[2,640]{1,0:T(2,128)S(1)}, u32[]{:S(2)}, u32[]{:S(2)}) %collective-permute-start.10) | collective-permute-done | bytes 5152 | tf_op jit(solution)/shard_map/ppermute | solution.py:170
  60.2 0.6 multiply_reduce_fusion.1
  60.8 0.5 slice.83
  61.3 0.7 %slice_reduce_fusion = f32[]{:T(128)} fusion(f32[2,640]{1,0:T(2,128)S(1)} %add.44), kind=kLoop, calls=%fused_computation.7 | loop fusion | flops 127 | bytes 516 | tf_op jit(solution)/shard_map/reduce_sum | solution.py:203
  62.7 0.0 copy-done.3
  62.7 0.6 divide_subtract_fusion.1
  64.0 0.0 copy-done.2
  64.0 0.6 divide_subtract_fusion
  (14 shorter events, 0.1 us)
Async XLA Ops:
  0.6 63.4 %copy-start.2 = (f32[2,2048]{1,0:T(2,128)S(1)}, f32[2,2048]{1,0:T(2,128)}, u32[]{:S(2)}) copy-start(f32[2,2048]{1,0:T(2,128)} %own.1) | copy-start | bytes 49156
  0.6 62.0 %copy-start.3 = (f32[2,512]{1,0:T(2,128)S(1)}, f32[2,512]{1,0:T(2,128)}, u32[]{:S(2)}) copy-start(f32[2,512]{1,0:T(2,128)} %param.7) | copy-start | bytes 12292
  1.4 5.2 %collective-permute-start = (f32[2,512]{1,0:T(2,128)S(1)}, f32[2,512]{1,0:T(2,128)S(1)}, u32[]{:S(2)}, u32[]{:S(2)}) collective-permute-start(f32[2,512]{1,0:T(2,128)S(1)} %get-tuple-element.18), channel_id=1, source_target_pairs={{0,8},{8,16},{16,24},{24,32},{32,40},{40,48},{48,56},{56,64},{64,7... | collective-permute-start | bytes 12296 | tf_op jit(solution)/shard_map/ppermute | solution.py:164
  1.4 5.2 %collective-permute-start.1 = (f32[2,512]{1,0:T(2,128)S(1)}, f32[2,512]{1,0:T(2,128)S(1)}, u32[]{:S(2)}, u32[]{:S(2)}) collective-permute-start(f32[2,512]{1,0:T(2,128)S(1)} %get-tuple-element.17), channel_id=1, source_target_pairs={{8,0},{16,8},{24,16},{32,24},{40,32},{48,40},{56,48},{64,56},{72,6... | collective-permute-start | bytes 12296 | tf_op jit(solution)/shard_map/ppermute | solution.py:164
  6.6 2.2 %copy-start = (bf16[1,2,512,2048]{3,2,1,0:T(8,128)(2,1)S(1)}, bf16[1,2,512,2048]{3,2,1,0:T(8,128)(2,1)}, u32[]{:S(2)}) copy-start(bf16[1,2,512,2048]{3,2,1,0:T(8,128)(2,1)} %spectra.1) | copy-start | bytes 12582916
  8.8 0.7 %copy-start.1 = (f32[2,2048]{1,0:T(2,128)S(1)}, f32[2,2048]{1,0:T(2,128)}, u32[]{:S(2)}) copy-start(f32[2,2048]{1,0:T(2,128)} %own.1) | copy-start | bytes 49156
  24.2 5.2 %collective-permute-start.2 = (f32[2,512]{1,0:T(2,128)S(1)}, f32[2,512]{1,0:T(2,128)S(1)}, u32[]{:S(2)}, u32[]{:S(2)}) collective-permute-start(f32[2,512]{1,0:T(2,128)S(1)} %slice.76), channel_id=1, source_target_pairs={{0,8},{8,16},{16,24},{24,32},{32,40},{40,48},{48,56},{56,64},{64,7... | collective-permute-start | bytes 12296 | tf_op jit(solution)/shard_map/ppermute | solution.py:164
  29.4 1.3 %collective-permute-start.3 = (f32[2,512]{1,0:T(2,128)S(1)}, f32[2,512]{1,0:T(2,128)S(1)}, u32[]{:S(2)}, u32[]{:S(2)}) collective-permute-start(f32[2,512]{1,0:T(2,128)S(1)} %get-tuple-element.16), channel_id=1, source_target_pairs={{8,0},{16,8},{24,16},{32,24},{40,32},{48,40},{56,48},{64,56},{72,6... | collective-permute-start | bytes 12296 | tf_op jit(solution)/shard_map/ppermute | solution.py:164
  30.7 3.9 %collective-permute-start.4 = (f32[2,2688]{1,0:T(2,128)S(1)}, f32[2,2688]{1,0:T(2,128)S(1)}, u32[]{:S(2)}, u32[]{:S(2)}) collective-permute-start(f32[2,2688]{1,0:T(2,128)S(1)} %pad_maximum_fusion), channel_id=1, source_target_pairs={{0,2},{1,3},{2,0},{3,1},{4,6},{5,7},{6,4},{7,5},{8,10},{9,11},{10,... | collective-permute-start | bytes 64520 | tf_op jit(solution)/shard_map/ppermute | solution.py:170
  34.6 5.1 %collective-permute-start.5 = (f32[2,2688]{1,0:T(2,128)S(1)}, f32[2,2688]{1,0:T(2,128)S(1)}, u32[]{:S(2)}, u32[]{:S(2)}) collective-permute-start(f32[2,2688]{1,0:T(2,128)S(1)} %fusion.1), channel_id=1, source_target_pairs={{0,6},{1,7},{2,4},{3,5},{4,2},{5,3},{6,0},{7,1},{8,14},{9,15},{10,... | collective-permute-start | bytes 64520 | tf_op jit(solution)/shard_map/ppermute | solution.py:170
  39.7 5.8 %collective-permute-start.6 = (f32[2,2688]{1,0:T(2,128)S(1)}, f32[2,2688]{1,0:T(2,128)S(1)}, u32[]{:S(2)}, u32[]{:S(2)}) collective-permute-start(f32[2,2688]{1,0:T(2,128)S(1)} %add.39), channel_id=1, source_target_pairs={{0,1},{1,0},{2,3},{3,2},{4,5},{5,4},{6,7},{7,6},{8,9},{9,8},{10,11... | collective-permute-start | bytes 64520 | tf_op jit(solution)/shard_map/ppermute | solution.py:170
  46.9 1.2 %collective-permute-start.7 = (f32[2,640]{1,0:T(2,128)S(1)}, f32[2,640]{1,0:T(2,128)S(1)}, u32[]{:S(2)}, u32[]{:S(2)}) collective-permute-start(f32[2,640]{1,0:T(2,128)S(1)} %scatter.4), channel_id=1, source_target_pairs={{0,8},{8,0},{16,24},{24,16},{32,40},{40,32},{48,56},{56,48},{64,72... | collective-permute-start | bytes 15368 | tf_op jit(solution)/shard_map/ppermute | solution.py:170
  48.1 3.6 %collective-permute-start.8 = (f32[2,640]{1,0:T(2,128)S(1)}, f32[2,640]{1,0:T(2,128)S(1)}, u32[]{:S(2)}, u32[]{:S(2)}) collective-permute-start(f32[2,640]{1,0:T(2,128)S(1)} %add.41), channel_id=1, source_target_pairs={{0,16},{8,24},{16,0},{24,8},{32,48},{40,56},{48,32},{56,40},{64,80... | collective-permute-start | bytes 15368 | tf_op jit(solution)/shard_map/ppermute | solution.py:170
  51.7 3.6 %collective-permute-start.9 = (f32[2,640]{1,0:T(2,128)S(1)}, f32[2,640]{1,0:T(2,128)S(1)}, u32[]{:S(2)}, u32[]{:S(2)}) collective-permute-start(f32[2,640]{1,0:T(2,128)S(1)} %add.42), channel_id=1, source_target_pairs={{0,32},{8,40},{16,48},{24,56},{32,0},{40,8},{48,16},{56,24},{64,96... | collective-permute-start | bytes 15368 | tf_op jit(solution)/shard_map/ppermute | solution.py:170
  55.4 4.8 %collective-permute-start.10 = (f32[2,640]{1,0:T(2,128)S(1)}, f32[2,640]{1,0:T(2,128)S(1)}, u32[]{:S(2)}, u32[]{:S(2)}) collective-permute-start(f32[2,640]{1,0:T(2,128)S(1)} %add.43), channel_id=1, source_target_pairs={{0,96},{8,104},{16,112},{24,120},{32,64},{40,72},{48,80},{56,88},{... | collective-permute-start | bytes 15368 | tf_op jit(solution)/shard_map/ppermute | solution.py:170

commit v2 on v0

v2 whole, which is shorter than its diff:
```python
import functools

import jax
import jax.numpy as jnp
from jax import lax
from jax.experimental import pallas as pl
from jax.experimental.pallas import tpu as pltpu
from jax.sharding import PartitionSpec as P

CHANNELS = 32768
LANES = 128
ROWS = 128
GROUP = 16
UNROLL = 2
VMEM_LIMIT = 24 * 1024 * 1024

filter_rate = 0.1
profile_rate = 0.1
epsilon = 1e-06


def skew(block, sign):
    width = block.shape[1]
    row = lax.broadcasted_iota(jnp.int32, block.shape, 0)
    for bit in (1, 2, 4):
        moved = pltpu.roll(block, bit if sign > 0 else width - bit, 1)
        block = jnp.where((row & bit) != 0, moved, block)
    return block


def gradient_kernel(
    factor, spectra, own_hbm, prof_hbm, prev, after, out,
    data, own, prof, fwd_re, fwd_im, bwd_re, bwd_im, up_re, up_im, down_re, down_im,
    q_re, q_im, part_re, part_im, err, block_sems, sems,
):
    owned = own.shape[1]
    harmonics = prof.shape[1]
    halo = harmonics
    width = owned + 2 * halo
    blocks = harmonics // ROWS
    edge = halo // LANES
    tiles = owned // LANES
    chan = lax.axis_index("chan")
    last = lax.axis_size("chan") - 1
    copies = [
        pltpu.make_async_copy(
            spectra.at[0, :, pl.ds(q * ROWS, ROWS), :],
            data.at[:, pl.ds(q * ROWS, ROWS), :],
            block_sems.at[q],
        )
        for q in range(blocks)
    ]
    own_copy = pltpu.make_async_copy(own_hbm, own, sems.at[0])
    prof_copy = pltpu.make_async_copy(prof_hbm, prof, sems.at[1])
    own_copy.start()
    prof_copy.start()
    for copy in copies:
        copy.start()

    for acc in (up_re, up_im):
        acc[:, halo - LANES : halo] = jnp.zeros((ROWS, LANES), jnp.float32)
        acc[:, halo + owned :] = jnp.zeros((ROWS, halo), jnp.float32)
    for acc in (down_re, down_im):
        acc[:, :halo] = jnp.zeros((ROWS, halo), jnp.float32)
        acc[:, halo + owned : halo + owned + LANES] = jnp.zeros((ROWS, LANES), jnp.float32)

    keep_low = jnp.where(chan == 0, 0.0, 1.0).astype(jnp.float32)
    keep_high = jnp.where(chan == last, 0.0, 1.0).astype(jnp.float32)
    own_copy.wait()
    reach = halo - ROWS
    for part, fwd, bwd in ((0, fwd_re, bwd_re), (1, fwd_im, bwd_im)):
        line = jnp.concatenate(
            [
                prev[part : part + 1, owned - halo :] * keep_low,
                own[part : part + 1, :],
                after[part : part + 1, :halo] * keep_high,
            ],
            axis=1,
        )
        base = jnp.broadcast_to(line, (8, width))
        right = skew(base, 1)
        left = skew(base, -1)
        for a in range(ROWS // 8):
            rows = pl.ds(8 * a, 8)
            moved = pltpu.roll(right, 8 * a, 1) if a else right
            bwd[rows, halo - reach : halo + owned] = moved[:, halo - reach : halo + owned]
            moved = pltpu.roll(left, width - 8 * a, 1) if a else left
            fwd[rows, halo : halo + owned + reach] = moved[:, halo : halo + owned + reach]

    prof_copy.wait()
    columns = jnp.transpose(
        jnp.concatenate([prof[...], jnp.zeros((6, harmonics), jnp.float32)], axis=0)
    )
    q_re[...] = jnp.broadcast_to(columns[:, 0:1], (harmonics, LANES))
    q_im[...] = jnp.broadcast_to(columns[:, 1:2], (harmonics, LANES))
    err[...] = jnp.zeros_like(err)

    for q in range(blocks):
        copies[q].wait()

        def group(index, carry, q=q):
            start = pl.multiple_of(index * GROUP, GROUP)
            rows = pl.ds(start, GROUP)
            krows = pl.ds(pl.multiple_of(q * ROWS + start, GROUP), GROUP)
            w_re = q_re[krows, :]
            w_im = q_im[krows, :]
            a_re = jnp.zeros((GROUP, LANES), jnp.float32)
            a_im = jnp.zeros((GROUP, LANES), jnp.float32)
            e_sum = jnp.zeros((GROUP, LANES), jnp.float32)
            for tile in range(tiles):
                cols = pl.ds(tile * LANES, LANES)
                above = pl.ds((edge + tile + q) * LANES, LANES)
                below = pl.ds((edge + tile - q) * LANES, LANES)
                s_re = data[0, krows, cols].astype(jnp.float32)
                s_im = data[1, krows, cols].astype(jnp.float32)
                f_re = fwd_re[rows, above]
                f_im = fwd_im[rows, above]
                b_re = bwd_re[rows, below]
                b_im = bwd_im[rows, below]
                p_re = f_re * b_re + f_im * b_im
                p_im = f_im * b_re - f_re * b_im
                r_re = s_re - (p_re * w_re - p_im * w_im)
                r_im = s_im - (p_re * w_im + p_im * w_re)
                e_sum = e_sum + (r_re * r_re + r_im * r_im)
                a_re = a_re + (r_re * p_re + r_im * p_im)
                a_im = a_im + (r_im * p_re - r_re * p_im)
                x_re = r_re * w_re + r_im * w_im
                x_im = r_im * w_re - r_re * w_im
                u_re = x_re * b_re - x_im * b_im
                u_im = x_re * b_im + x_im * b_re
                d_re = x_re * f_re + x_im * f_im
                d_im = x_re * f_im - x_im * f_re
                if q == 0:
                    up_re[rows, above] = u_re
                    up_im[rows, above] = u_im
                    down_re[rows, below] = d_re
                    down_im[rows, below] = d_im
                else:
                    up_re[rows, above] += u_re
                    up_im[rows, above] += u_im
                    down_re[rows, below] += d_re
                    down_im[rows, below] += d_im
            part_re[krows, :] = a_re
            part_im[krows, :] = a_im
            err[...] += e_sum
            return carry

        lax.fori_loop(0, ROWS // GROUP, group, 0, unroll=UNROLL)

    ones = jnp.ones((8, LANES), jnp.float32)
    span = (owned + halo) // 2
    for part, up, down, sums in (
        (0, up_re, down_re, part_re),
        (1, up_im, down_im, part_im),
    ):
        raised = []
        lowered = []
        for half in range(2):
            first = halo - LANES + half * span
            total = up[0:8, first : first + span + LANES]
            for a in range(1, ROWS // 8):
                piece = up[8 * a : 8 * a + 8, first : first + span + LANES]
                total = total + pltpu.roll(piece, 8 * a, 1)
            raised.append(jnp.sum(skew(total, 1)[:, LANES:], axis=0, keepdims=True))
            first = half * span
            total = down[0:8, first : first + span + LANES]
            for a in range(1, ROWS // 8):
                piece = down[8 * a : 8 * a + 8, first : first + span + LANES]
                total = total + pltpu.roll(piece, span + LANES - 8 * a, 1)
            lowered.append(jnp.sum(skew(total, -1)[:, :span], axis=0, keepdims=True))
        raised = jnp.concatenate(raised, axis=1) * factor
        lowered = jnp.concatenate(lowered, axis=1) * factor
        row = slice(part, part + 1)
        out[row, 0:halo] = lowered[:, :halo] * keep_low
        out[row, halo : halo + owned] = lowered[:, halo:] + raised[:, :owned]
        out[row, halo + owned : width] = raised[:, owned:] * keep_high
        reduced = lax.dot_general(
            ones,
            sums[...],
            (((1,), (1,)), ((), ())),
            precision=lax.Precision.HIGHEST,
            preferred_element_type=jnp.float32,
        )
        out[row, width : width + harmonics] = factor * reduced[0:1, :]
    out[0:1, width + harmonics :] = jnp.sum(err[...], axis=0, keepdims=True)
    out[1:2, width + harmonics :] = jnp.zeros((1, LANES), jnp.float32)


def local_gradients(factor, spectra, own, prof, prev, after):
    harmonics = prof.shape[1]
    owned = own.shape[1]
    width = owned + 2 * harmonics
    table = pltpu.VMEM((ROWS, width), jnp.float32)
    column = pltpu.VMEM((harmonics, LANES), jnp.float32)
    anywhere = pl.BlockSpec(memory_space=pltpu.HBM)
    inside = pl.BlockSpec(memory_space=pltpu.VMEM)
    return pl.pallas_call(
        functools.partial(gradient_kernel, factor),
        in_specs=[anywhere, anywhere, anywhere, inside, inside],
        out_specs=inside,
        out_shape=jax.ShapeDtypeStruct((2, width + harmonics + LANES), jnp.float32),
        scratch_shapes=[
            pltpu.VMEM((2, harmonics, owned), jnp.bfloat16),
            pltpu.VMEM((2, owned), jnp.float32),
            pltpu.VMEM((2, harmonics), jnp.float32),
        ]
        + [table] * 8
        + [column] * 4
        + [
            pltpu.VMEM((GROUP, LANES), jnp.float32),
            pltpu.SemaphoreType.DMA((harmonics // ROWS,)),
            pltpu.SemaphoreType.DMA((2,)),
        ],
        compiler_params=pltpu.CompilerParams(vmem_limit_bytes=VMEM_LIMIT),
    )(*(pltpu.with_memory_space_constraint(x, pltpu.HBM) for x in (spectra, own, prof)), prev, after)


def final_kernel(weight, sums, grads, low_add, high_add, filt, prof, filt_out, prof_out, misfit):
    harmonics = prof.shape[1]
    owned = filt.shape[1]
    halo = harmonics
    squares = jnp.sum(sums[:, harmonics + LANES :])
    scale = filter_rate / jnp.sqrt(jnp.full((2, LANES), squares) / (2 * CHANNELS) + epsilon)
    scale = scale[:, 0:1]
    low = grads[:, halo : 2 * halo] + low_add[:, halo:]
    middle = grads[:, 2 * halo : owned]
    high = grads[:, owned : owned + halo] + high_add[:, :halo]
    filt_out[:, :halo] = filt[:, :halo] - scale * low
    filt_out[:, halo : owned - halo] = filt[:, halo : owned - halo] - scale * middle
    filt_out[:, owned - halo :] = filt[:, owned - halo :] - scale * high
    grad = sums[:, :harmonics]
    mean = jnp.sum(grad * grad) / (2 * harmonics)
    rate = profile_rate / jnp.sqrt(jnp.full((2, LANES), mean) + epsilon)
    prof_out[...] = prof[...] - rate[:, 0:1] * grad
    total = jnp.sum(sums[:, harmonics : harmonics + LANES])
    misfit[0] = total * (weight / CHANNELS)


def update(weight, sums, grads, low_add, high_add, filt, prof):
    inside = pl.BlockSpec(memory_space=pltpu.VMEM)
    return pl.pallas_call(
        functools.partial(final_kernel, weight),
        in_specs=[inside] * 6,
        out_specs=[inside, inside, pl.BlockSpec(memory_space=pltpu.SMEM)],
        out_shape=[
            jax.ShapeDtypeStruct(filt.shape, jnp.float32),
            jax.ShapeDtypeStruct(prof.shape, jnp.float32),
            jax.ShapeDtypeStruct((1,), jnp.float32),
        ],
        compiler_params=pltpu.CompilerParams(vmem_limit_bytes=2 * 1024 * 1024),
    )(sums, grads, low_add, high_add, filt, prof)


def fold(values):
    total = values[:, :LANES]
    for start in range(LANES, values.shape[1], LANES):
        total = total + values[:, start : start + LANES]
    return total


def swap(values, axis, mask):
    count = lax.axis_size(axis)
    return lax.ppermute(values, axis, [(i, i ^ mask) for i in range(count)])


def neighbours(to_next, to_previous, axis):
    count = lax.axis_size(axis)
    ahead = [(i, (i + 1) % count) for i in range(count)]
    back = [(target, source) for source, target in ahead]
    return lax.ppermute(to_next, axis, ahead), lax.ppermute(to_previous, axis, back)


def join_blocks(sums, low_edge, high_edge, axis, masks):
    chan = lax.axis_index(axis)
    size = sums.shape[1]
    span = low_edge.shape[1]
    low_add = jnp.zeros_like(low_edge)
    high_add = jnp.zeros_like(high_edge)
    for step, mask in enumerate(masks):
        is_low = (chan >> step) & 1 == 0
        place = chan & ((1 << step) - 1)
        if step < len(masks) - 1:
            got = swap(jnp.concatenate([sums, low_edge, high_edge], axis=1), axis, mask)
            facing = jnp.where(is_low, got[:, size : size + span], got[:, size + span :])
        else:
            got = swap(jnp.concatenate([sums, jnp.where(is_low, high_edge, low_edge)], axis=1), axis, mask)
            facing = got[:, size:]
        mine = jnp.where(is_low, high_edge, low_edge)
        cross = 2.0 * fold(mine * facing)
        sums = sums + got[:, :size]
        sums = jnp.concatenate([sums[:, : size - LANES], sums[:, size - LANES :] + cross], axis=1)
        high_add = jnp.where(is_low & (place == (1 << step) - 1), facing, high_add)
        low_add = jnp.where(~is_low & (place == 0), facing, low_add)
        if step < len(masks) - 1:
            low_edge = jnp.where(is_low, low_edge, got[:, size : size + span])
            high_edge = jnp.where(is_low, got[:, size + span :], high_edge)
    return sums, low_add, high_add


def on_device(spectra, filter_init, profile_init):
    harmonics = profile_init.shape[1]
    owned = filter_init.shape[1]
    width = owned + 2 * harmonics
    weight = 1.0 / (lax.axis_size("sub") * spectra.shape[0] * harmonics)
    prev, after = neighbours(filter_init, filter_init, "chan")
    local = local_gradients(-2.0 * weight, spectra, filter_init, profile_init, prev, after)
    for mask in (2, 6, 1):
        local = local + swap(local, "sub", mask)
    grads = local[:, :width]
    sums = jnp.concatenate([local[:, width:], fold(grads * grads)], axis=1)
    sums, low_add, high_add = join_blocks(
        sums, grads[:, : 2 * harmonics], grads[:, owned:], "chan", (1, 2, 4, 12)
    )
    return tuple(update(weight, sums, grads, low_add, high_add, filter_init, profile_init))


def solution(mesh):
    return jax.shard_map(
        on_device,
        mesh=mesh,
        in_specs=(P("sub", None, None, "chan"), P(None, "chan"), P()),
        out_specs=(P(None, "chan"), P(), P()),
        check_vma=False,
    )
```

time: 450 us -> 50.7 us (0.11)
  the two profiles are of different devices: /device:TPU:1 before, /device:TPU:0 now
where the time goes in v2:
time: 50.7 us; the launch traced here: 50.5 us
  waiting for transfers between devices  19.4 us (38%)
  starting transfers between devices  15.2 us (30%)
  Pallas kernels  14.8 us (29%)
  between operations  0.84 us (2%)
    ppermute x7, waiting for transfers between devices, swap(): return lax.ppermute(values, axis, [(i, i ^ mask) for i in range(count)])  17.8 us
    pallas_call x1, Pallas kernels, local_gradients(): pl.pallas_call(functools.partial(gradient_kernel, factor), in_specs=[anyw...  14 us
    ppermute x7, starting transfers between devices, swap(): return lax.ppermute(values, axis, [(i, i ^ mask) for i in range(count)])  11.2 us
    ppermute x1, starting transfers between devices, neighbours(): lax.ppermute(to_previous, axis, back)  3.96 us
    ppermute x1, waiting for transfers between devices, neighbours(): lax.ppermute(to_next, axis, ahead)  1.55 us
  transfers between devices with their start and end apart: 9, of which 9 were waited for; matrix products, arithmetic and copies ran while one was open for 0% of the time, Pallas kernels for 0%

profile of v2, /device:TPU:0, one launch (start us, length us, event | category | flops | bytes accessed | tf_op | source)
XLA Modules:
  0.0 50.5 jit_solution(2600118922490773209)
XLA Ops:
  0.6 0.0 copy-start
  0.6 0.0 copy-start.1
  0.7 0.1 collective-permute-start
  0.7 4.0 %collective-permute-start.1 = (f32[2,2048]{1,0:T(2,128)}, f32[2,2048]{1,0:T(2,128)S(1)}, u32[]{:S(2)}, u32[]{:S(2)}) collective-permute-start(f32[2,2048]{1,0:T(2,128)} %filt.1), channel_id=1, source_target_pairs={{8,0},{16,8},{24,16},{32,24},{40,32},{48,40},{56,48},{64,56},{72,6... | collective-permute-start | bytes 49160 | tf_op jit(solution)/shard_map/ppermute | solution.py:270
  4.7 1.6 %collective-permute-done.prev = f32[2,2048]{1,0:T(2,128)S(1)} collective-permute-done((f32[2,2048]{1,0:T(2,128)}, f32[2,2048]{1,0:T(2,128)S(1)}, u32[]{:S(2)}, u32[]{:S(2)}) %collective-permute-start) | collective-permute-done | bytes 16416 | tf_op jit(solution)/shard_map/ppermute | solution.py:270
  6.2 0.1 collective-permute-done.1.after
  6.3 14.0 %shard_map.58 = f32[2,3712]{1,0:T(2,128)S(1)} custom-call(bf16[1,2,512,2048]{3,2,1,0:T(8,128)(2,1)} %spectra.1, f32[2,2048]{1,0:T(2,128)} %filt.1, f32[2,512]{1,0:T(2,128)} %prof.1, f32[2,2048]{1,0:T(2,128)S(1)} %collective-permute-done.prev, f32[2,2048]{1,0:T(2,128)S(1)} %collective-permute-done.1.after), custom_call_target="tpu_custom_call" | custom-call | tf_op jit(solution)/shard_map/pallas_call | solution.py:197
  20.4 1.6 %collective-permute-start.2 = (f32[2,3712]{1,0:T(2,128)S(1)}, f32[2,3712]{1,0:T(2,128)S(1)}, u32[]{:S(2)}, u32[]{:S(2)}) collective-permute-start(f32[2,3712]{1,0:T(2,128)S(1)} %shard_map.58), channel_id=1, source_target_pairs={{0,2},{1,3},{2,0},{3,1},{4,6},{5,7},{6,4},{7,5},{8,10},{9,11},{10,... | collective-permute-start | bytes 89096 | tf_op jit(solution)/shard_map/ppermute | solution.py:263
  21.9 2.4 %collective-permute-done.2 = f32[2,3712]{1,0:T(2,128)S(1)} collective-permute-done((f32[2,3712]{1,0:T(2,128)S(1)}, f32[2,3712]{1,0:T(2,128)S(1)}, u32[]{:S(2)}, u32[]{:S(2)}) %collective-permute-start.2) | collective-permute-done | bytes 29728 | tf_op jit(solution)/shard_map/ppermute | solution.py:263
  24.3 2.8 %collective-permute-start.3 = (f32[2,3712]{1,0:T(2,128)S(1)}, f32[2,3712]{1,0:T(2,128)S(1)}, u32[]{:S(2)}, u32[]{:S(2)}) collective-permute-start(f32[2,3712]{1,0:T(2,128)S(1)} %add.186), channel_id=1, source_target_pairs={{0,6},{1,7},{2,4},{3,5},{4,2},{5,3},{6,0},{7,1},{8,14},{9,15},{10,... | collective-permute-start | bytes 89096 | tf_op jit(solution)/shard_map/ppermute | solution.py:263
  27.2 2.3 %collective-permute-done.3 = f32[2,3712]{1,0:T(2,128)S(1)} collective-permute-done((f32[2,3712]{1,0:T(2,128)S(1)}, f32[2,3712]{1,0:T(2,128)S(1)}, u32[]{:S(2)}, u32[]{:S(2)}) %collective-permute-start.3) | collective-permute-done | bytes 29728 | tf_op jit(solution)/shard_map/ppermute | solution.py:263
  29.5 3.9 %collective-permute-start.4 = (f32[2,3712]{1,0:T(2,128)S(1)}, f32[2,3712]{1,0:T(2,128)S(1)}, u32[]{:S(2)}, u32[]{:S(2)}) collective-permute-start(f32[2,3712]{1,0:T(2,128)S(1)} %add.187), channel_id=1, source_target_pairs={{0,1},{1,0},{2,3},{3,2},{4,5},{5,4},{6,7},{7,6},{8,9},{9,8},{10,11... | collective-permute-start | bytes 89096 | tf_op jit(solution)/shard_map/ppermute | solution.py:263
  33.5 1.9 %collective-permute-done.4 = f32[2,3712]{1,0:T(2,128)S(1)} collective-permute-done((f32[2,3712]{1,0:T(2,128)S(1)}, f32[2,3712]{1,0:T(2,128)S(1)}, u32[]{:S(2)}, u32[]{:S(2)}) %collective-permute-start.4) | collective-permute-done | bytes 29728 | tf_op jit(solution)/shard_map/ppermute | solution.py:263
  35.4 0.1 collective-permute-start.5
  35.5 1.2 %collective-permute-done.5 = f32[2,2816]{1,0:T(2,128)S(1)} collective-permute-done((f32[2,2816]{1,0:T(2,128)S(1)}, f32[2,2816]{1,0:T(2,128)S(1)}, u32[]{:S(2)}, u32[]{:S(2)}) %collective-permute-start.5) | collective-permute-done | bytes 22560 | tf_op jit(solution)/shard_map/ppermute | solution.py:263
  36.8 0.1 collective-permute-start.6
  36.9 3.8 %collective-permute-done.6 = f32[2,2816]{1,0:T(2,128)S(1)} collective-permute-done((f32[2,2816]{1,0:T(2,128)S(1)}, f32[2,2816]{1,0:T(2,128)S(1)}, u32[]{:S(2)}, u32[]{:S(2)}) %collective-permute-start.6) | collective-permute-done | bytes 22560 | tf_op jit(solution)/shard_map/ppermute | solution.py:263
  40.7 0.6 %collective-permute-start.7 = (f32[2,2816]{1,0:T(2,128)S(1)}, f32[2,2816]{1,0:T(2,128)S(1)}, u32[]{:S(2)}, u32[]{:S(2)}) collective-permute-start(f32[2,2816]{1,0:T(2,128)S(1)} %pad_maximum_fusion.2), channel_id=1, source_target_pairs={{0,32},{8,40},{16,48},{24,56},{32,0},{40,8},{48,16},{56,24},{64,96... | collective-permute-start | bytes 67592 | tf_op jit(solution)/shard_map/ppermute | solution.py:263
  41.3 3.3 %collective-permute-done.7 = f32[2,2816]{1,0:T(2,128)S(1)} collective-permute-done((f32[2,2816]{1,0:T(2,128)S(1)}, f32[2,2816]{1,0:T(2,128)S(1)}, u32[]{:S(2)}, u32[]{:S(2)}) %collective-permute-start.7) | collective-permute-done | bytes 22560 | tf_op jit(solution)/shard_map/ppermute | solution.py:263
  44.7 2.0 %collective-permute-start.8 = (f32[2,1792]{1,0:T(2,128)S(1)}, f32[2,1792]{1,0:T(2,128)S(1)}, u32[]{:S(2)}, u32[]{:S(2)}) collective-permute-start(f32[2,1792]{1,0:T(2,128)S(1)} %pad_maximum_fusion.3), channel_id=1, source_target_pairs={{0,96},{8,104},{16,112},{24,120},{32,64},{40,72},{48,80},{56,88},{... | collective-permute-start | bytes 43016 | tf_op jit(solution)/shard_map/ppermute | solution.py:263
  46.7 3.0 %collective-permute-done.8 = f32[2,1792]{1,0:T(2,128)S(1)} collective-permute-done((f32[2,1792]{1,0:T(2,128)S(1)}, f32[2,1792]{1,0:T(2,128)S(1)}, u32[]{:S(2)}, u32[]{:S(2)}) %collective-permute-start.8) | collective-permute-done | bytes 14368 | tf_op jit(solution)/shard_map/ppermute | solution.py:263
  49.8 0.0 copy-done
  49.8 0.0 copy-done.1
  49.8 0.8 %shard_map.59 = (f32[2,2048]{1,0:T(2,128)}, f32[2,512]{1,0:T(2,128)}, f32[1]{0:T(128)}) custom-call(f32[2,768]{1,0:T(2,128)S(1)} %pad_maximum_fusion.4.sums, f32[2,3072]{1,0:T(2,128)S(1)} %get-tuple-element.15.grads, f32[2,1024]{1,0:T(2,128)S(1)} %get-tuple-element.8.low_add, f32[2,1024]{1,0:T(2,128)S(1)} %get-tuple-element.7.high_add, ...), custom_call_target="tpu_custom_call" | custom-call | tf_op jit(solution)/shard_map/pallas_call | solution.py:241
  (28 shorter events, 0.3 us)
Async XLA Ops:
  0.6 49.1 %copy-start = (f32[2,2048]{1,0:T(2,128)S(1)}, f32[2,2048]{1,0:T(2,128)}, u32[]{:S(2)}) copy-start(f32[2,2048]{1,0:T(2,128)} %filt.1) | copy-start | bytes 49156
  0.6 49.1 %copy-start.1 = (f32[2,512]{1,0:T(2,128)S(1)}, f32[2,512]{1,0:T(2,128)}, u32[]{:S(2)}) copy-start(f32[2,512]{1,0:T(2,128)} %prof.1) | copy-start | bytes 12292
  0.7 5.6 %collective-permute-start = (f32[2,2048]{1,0:T(2,128)}, f32[2,2048]{1,0:T(2,128)S(1)}, u32[]{:S(2)}, u32[]{:S(2)}) collective-permute-start(f32[2,2048]{1,0:T(2,128)} %filt.1), channel_id=1, source_target_pairs={{0,8},{8,16},{16,24},{24,32},{32,40},{40,48},{48,56},{56,64},{64,7... | collective-permute-start | bytes 49160 | tf_op jit(solution)/shard_map/ppermute | solution.py:270
  0.7 5.6 %collective-permute-start.1 = (f32[2,2048]{1,0:T(2,128)}, f32[2,2048]{1,0:T(2,128)S(1)}, u32[]{:S(2)}, u32[]{:S(2)}) collective-permute-start(f32[2,2048]{1,0:T(2,128)} %filt.1), channel_id=1, source_target_pairs={{8,0},{16,8},{24,16},{32,24},{40,32},{48,40},{56,48},{64,56},{72,6... | collective-permute-start | bytes 49160 | tf_op jit(solution)/shard_map/ppermute | solution.py:270
  20.4 4.0 %collective-permute-start.2 = (f32[2,3712]{1,0:T(2,128)S(1)}, f32[2,3712]{1,0:T(2,128)S(1)}, u32[]{:S(2)}, u32[]{:S(2)}) collective-permute-start(f32[2,3712]{1,0:T(2,128)S(1)} %shard_map.58), channel_id=1, source_target_pairs={{0,2},{1,3},{2,0},{3,1},{4,6},{5,7},{6,4},{7,5},{8,10},{9,11},{10,... | collective-permute-start | bytes 89096 | tf_op jit(solution)/shard_map/ppermute | solution.py:263
  24.3 5.2 %collective-permute-start.3 = (f32[2,3712]{1,0:T(2,128)S(1)}, f32[2,3712]{1,0:T(2,128)S(1)}, u32[]{:S(2)}, u32[]{:S(2)}) collective-permute-start(f32[2,3712]{1,0:T(2,128)S(1)} %add.186), channel_id=1, source_target_pairs={{0,6},{1,7},{2,4},{3,5},{4,2},{5,3},{6,0},{7,1},{8,14},{9,15},{10,... | collective-permute-start | bytes 89096 | tf_op jit(solution)/shard_map/ppermute | solution.py:263
  29.5 5.8 %collective-permute-start.4 = (f32[2,3712]{1,0:T(2,128)S(1)}, f32[2,3712]{1,0:T(2,128)S(1)}, u32[]{:S(2)}, u32[]{:S(2)}) collective-permute-start(f32[2,3712]{1,0:T(2,128)S(1)} %add.187), channel_id=1, source_target_pairs={{0,1},{1,0},{2,3},{3,2},{4,5},{5,4},{6,7},{7,6},{8,9},{9,8},{10,11... | collective-permute-start | bytes 89096 | tf_op jit(solution)/shard_map/ppermute | solution.py:263
  35.4 1.3 %collective-permute-start.5 = (f32[2,2816]{1,0:T(2,128)S(1)}, f32[2,2816]{1,0:T(2,128)S(1)}, u32[]{:S(2)}, u32[]{:S(2)}) collective-permute-start(f32[2,2816]{1,0:T(2,128)S(1)} %pad_maximum_fusion), channel_id=1, source_target_pairs={{0,8},{8,0},{16,24},{24,16},{32,40},{40,32},{48,56},{56,48},{64,72... | collective-permute-start | bytes 67592 | tf_op jit(solution)/shard_map/ppermute | solution.py:263
  36.8 3.9 %collective-permute-start.6 = (f32[2,2816]{1,0:T(2,128)S(1)}, f32[2,2816]{1,0:T(2,128)S(1)}, u32[]{:S(2)}, u32[]{:S(2)}) collective-permute-start(f32[2,2816]{1,0:T(2,128)S(1)} %pad_maximum_fusion.1), channel_id=1, source_target_pairs={{0,16},{8,24},{16,0},{24,8},{32,48},{40,56},{48,32},{56,40},{64,80... | collective-permute-start | bytes 67592 | tf_op jit(solution)/shard_map/ppermute | solution.py:263
  40.7 3.9 %collective-permute-start.7 = (f32[2,2816]{1,0:T(2,128)S(1)}, f32[2,2816]{1,0:T(2,128)S(1)}, u32[]{:S(2)}, u32[]{:S(2)}) collective-permute-start(f32[2,2816]{1,0:T(2,128)S(1)} %pad_maximum_fusion.2), channel_id=1, source_target_pairs={{0,32},{8,40},{16,48},{24,56},{32,0},{40,8},{48,16},{56,24},{64,96... | collective-permute-start | bytes 67592 | tf_op jit(solution)/shard_map/ppermute | solution.py:263
  44.7 5.0 %collective-permute-start.8 = (f32[2,1792]{1,0:T(2,128)S(1)}, f32[2,1792]{1,0:T(2,128)S(1)}, u32[]{:S(2)}, u32[]{:S(2)}) collective-permute-start(f32[2,1792]{1,0:T(2,128)S(1)} %pad_maximum_fusion.3), channel_id=1, source_target_pairs={{0,96},{8,104},{16,112},{24,120},{32,64},{40,72},{48,80},{56,88},{... | collective-permute-start | bytes 43016 | tf_op jit(solution)/shard_map/ppermute | solution.py:263

commit v3 on v2

--- a/solution.py
+++ b/solution.py
@@ -12,7 +12,7 @@
 ROWS = 128
 GROUP = 16
 UNROLL = 2
-VMEM_LIMIT = 24 * 1024 * 1024
+VMEM_LIMIT = 28 * 1024 * 1024
 
 filter_rate = 0.1
 profile_rate = 0.1
@@ -29,9 +29,10 @@
 
 
 def gradient_kernel(
-    factor, spectra, own_hbm, prof_hbm, prev, after, out,
-    data, own, prof, fwd_re, fwd_im, bwd_re, bwd_im, up_re, up_im, down_re, down_im,
-    q_re, q_im, part_re, part_im, err, block_sems, sems,
+    factor, spectra, prof_hbm, own, prev, after, out,
+    data, prof, fwd_re, fwd_im, fwd_sum, fwd_dif, bwd_re, bwd_sum, bwd_dif,
+    up_re, up_im, down_re, down_im,
+    unit_re, unit_im, size, part_re, part_im, err, block_sems, prof_sem,
 ):
     owned = own.shape[1]
     harmonics = prof.shape[1]
@@ -50,9 +51,7 @@
         )
         for q in range(blocks)
     ]
-    own_copy = pltpu.make_async_copy(own_hbm, own, sems.at[0])
-    prof_copy = pltpu.make_async_copy(prof_hbm, prof, sems.at[1])
-    own_copy.start()
+    prof_copy = pltpu.make_async_copy(prof_hbm, prof, prof_sem)
     prof_copy.start()
     for copy in copies:
         copy.start()
@@ -66,10 +65,9 @@
 
     keep_low = jnp.where(chan == 0, 0.0, 1.0).astype(jnp.float32)
     keep_high = jnp.where(chan == last, 0.0, 1.0).astype(jnp.float32)
-    own_copy.wait()
     reach = halo - ROWS
-    for part, fwd, bwd in ((0, fwd_re, bwd_re), (1, fwd_im, bwd_im)):
-        line = jnp.concatenate(
+    lines = [
+        jnp.concatenate(
             [
                 prev[part : part + 1, owned - halo :] * keep_low,
                 own[part : part + 1, :],
@@ -77,22 +75,38 @@
             ],
             axis=1,
         )
-        base = jnp.broadcast_to(line, (8, width))
-        right = skew(base, 1)
-        left = skew(base, -1)
-        for a in range(ROWS // 8):
-            rows = pl.ds(8 * a, 8)
-            moved = pltpu.roll(right, 8 * a, 1) if a else right
-            bwd[rows, halo - reach : halo + owned] = moved[:, halo - reach : halo + owned]
-            moved = pltpu.roll(left, width - 8 * a, 1) if a else left
-            fwd[rows, halo : halo + owned + reach] = moved[:, halo : halo + owned + reach]
+        for part in range(2)
+    ]
+    bases = [jnp.broadcast_to(line, (8, width)) for line in lines]
+    rights = [skew(base, 1) for base in bases]
+    lefts = [skew(base, -1) for base in bases]
+    behind = slice(halo - reach, halo + owned)
+    ahead = slice(halo, halo + owned + reach)
+    for a in range(ROWS // 8):
+        rows = pl.ds(8 * a, 8)
+        re, im = ((pltpu.roll(x, 8 * a, 1) if a else x)[:, behind] for x in rights)
+        bwd_re[rows, behind] = re
+        bwd_sum[rows, behind] = re + im
+        bwd_dif[rows, behind] = re - im
+        re, im = ((pltpu.roll(x, width - 8 * a, 1) if a else x)[:, ahead] for x in lefts)
+        fwd_re[rows, ahead] = re
+        fwd_im[rows, ahead] = im
+        fwd_sum[rows, ahead] = re + im
+        fwd_dif[rows, ahead] = re - im
 
     prof_copy.wait()
+    prof_re = prof[0:1, :]
+    prof_im = prof[1:2, :]
+    length = jnp.sqrt(prof_re * prof_re + prof_im * prof_im)
+    present = length > 0.0
+    divisor = jnp.where(present, length, 1.0)
+    turn_re = jnp.where(present, prof_re / divisor, 1.0)
+    turn_im = jnp.where(present, prof_im / divisor, 0.0)
     columns = jnp.transpose(
-        jnp.concatenate([prof[...], jnp.zeros((6, harmonics), jnp.float32)], axis=0)
+        jnp.concatenate([turn_re, turn_im, length, jnp.zeros((5, harmonics), jnp.float32)], axis=0)
     )
-    q_re[...] = jnp.broadcast_to(columns[:, 0:1], (harmonics, LANES))
-    q_im[...] = jnp.broadcast_to(columns[:, 1:2], (harmonics, LANES))
+    for index, table in enumerate((unit_re, unit_im, size)):
+        table[...] = jnp.broadcast_to(columns[:, index : index + 1], (harmonics, LANES))
     err[...] = jnp.zeros_like(err)
 
     for q in range(blocks):
@@ -102,8 +116,9 @@
             start = pl.multiple_of(index * GROUP, GROUP)
             rows = pl.ds(start, GROUP)
             krows = pl.ds(pl.multiple_of(q * ROWS + start, GROUP), GROUP)
-            w_re = q_re[krows, :]
-            w_im = q_im[krows, :]
+            w_re = unit_re[krows, :]
+            w_im = unit_im[krows, :]
+            mag = size[krows, :]
             a_re = jnp.zeros((GROUP, LANES), jnp.float32)
             a_im = jnp.zeros((GROUP, LANES), jnp.float32)
             e_sum = jnp.zeros((GROUP, LANES), jnp.float32)
@@ -113,23 +128,30 @@
                 below = pl.ds((edge + tile - q) * LANES, LANES)
                 s_re = data[0, krows, cols].astype(jnp.float32)
                 s_im = data[1, krows, cols].astype(jnp.float32)
-                f_re = fwd_re[rows, above]
+                t_re = s_re * w_re + s_im * w_im
+                t_im = s_im * w_re - s_re * w_im
+                f_sum = fwd_sum[rows, above]
                 f_im = fwd_im[rows, above]
                 b_re = bwd_re[rows, below]
-                b_im = bwd_im[rows, below]
-                p_re = f_re * b_re + f_im * b_im
-                p_im = f_im * b_re - f_re * b_im
-                r_re = s_re - (p_re * w_re - p_im * w_im)
-                r_im = s_im - (p_re * w_im + p_im * w_re)
+                b_sum = bwd_sum[rows, below]
+                b_dif = bwd_dif[rows, below]
+                shared = b_re * f_sum
+                p_re = shared - f_im * b_dif
+                p_im = shared - fwd_re[rows, above] * b_sum
+                r_re = t_re - mag * p_re
+                r_im = t_im - mag * p_im
                 e_sum = e_sum + (r_re * r_re + r_im * r_im)
                 a_re = a_re + (r_re * p_re + r_im * p_im)
                 a_im = a_im + (r_im * p_re - r_re * p_im)
-                x_re = r_re * w_re + r_im * w_im
-                x_im = r_im * w_re - r_re * w_im
-                u_re = x_re * b_re - x_im * b_im
-                u_im = x_re * b_im + x_im * b_re
-                d_re = x_re * f_re + x_im * f_im
-                d_im = x_re * f_im - x_im * f_re
+                x_re = mag * r_re
+                x_im = mag * r_im
+                x_sum = x_re + x_im
+                shared = b_re * x_sum
+                u_re = shared - x_im * b_sum
+                u_im = shared - x_re * b_dif
+                shared = f_im * x_sum
+                d_re = shared + x_re * fwd_dif[rows, above]
+                d_im = shared - x_im * f_sum
                 if q == 0:
                     up_re[rows, above] = u_re
                     up_im[rows, above] = u_im
@@ -149,39 +171,47 @@
 
     ones = jnp.ones((8, LANES), jnp.float32)
     span = (owned + halo) // 2
-    for part, up, down, sums in (
-        (0, up_re, down_re, part_re),
-        (1, up_im, down_im, part_im),
-    ):
-        raised = []
-        lowered = []
+    raised = []
+    lowered = []
+    for up, down in ((up_re, down_re), (up_im, down_im)):
         for half in range(2):
             first = halo - LANES + half * span
             total = up[0:8, first : first + span + LANES]
             for a in range(1, ROWS // 8):
                 piece = up[8 * a : 8 * a + 8, first : first + span + LANES]
                 total = total + pltpu.roll(piece, 8 * a, 1)
-            raised.append(jnp.sum(skew(total, 1)[:, LANES:], axis=0, keepdims=True))
+            raised.append(total)
             first = half * span
             total = down[0:8, first : first + span + LANES]
             for a in range(1, ROWS // 8):
                 piece = down[8 * a : 8 * a + 8, first : first + span + LANES]
                 total = total + pltpu.roll(piece, span + LANES - 8 * a, 1)
-            lowered.append(jnp.sum(skew(total, -1)[:, :span], axis=0, keepdims=True))
-        raised = jnp.concatenate(raised, axis=1) * factor
-        lowered = jnp.concatenate(lowered, axis=1) * factor
+            lowered.append(total)
+    raised = skew(jnp.concatenate(raised, axis=0), 1)[:, LANES:]
+    lowered = skew(jnp.concatenate(lowered, axis=0), -1)[:, :span]
+    raised = factor * jnp.sum(raised.reshape(4, 8, span), axis=1)
+    lowered = factor * jnp.sum(lowered.reshape(4, 8, span), axis=1)
+    for part in range(2):
         row = slice(part, part + 1)
-        out[row, 0:halo] = lowered[:, :halo] * keep_low
-        out[row, halo : halo + owned] = lowered[:, halo:] + raised[:, :owned]
-        out[row, halo + owned : width] = raised[:, owned:] * keep_high
-        reduced = lax.dot_general(
+        rise = jnp.concatenate([raised[2 * part + i : 2 * part + i + 1] for i in range(2)], axis=1)
+        fall = jnp.concatenate([lowered[2 * part + i : 2 * part + i + 1] for i in range(2)], axis=1)
+        out[row, 0:halo] = fall[:, :halo] * keep_low
+        out[row, halo : halo + owned] = fall[:, halo:] + rise[:, :owned]
+        out[row, halo + owned : width] = rise[:, owned:] * keep_high
+    turned = [
+        lax.dot_general(
             ones,
             sums[...],
             (((1,), (1,)), ((), ())),
             precision=lax.Precision.HIGHEST,
             preferred_element_type=jnp.float32,
-        )
-        out[row, width : width + harmonics] = factor * reduced[0:1, :]
+        )[0:1, :]
+        for sums in (part_re, part_im)
+    ]
+    line = turned[0] * turn_re - turned[1] * turn_im
+    out[0:1, width : width + harmonics] = factor * line
+    line = turned[0] * turn_im + turned[1] * turn_re
+    out[1:2, width : width + harmonics] = factor * line
     out[0:1, width + harmonics :] = jnp.sum(err[...], axis=0, keepdims=True)
     out[1:2, width + harmonics :] = jnp.zeros((1, LANES), jnp.float32)
 
@@ -196,23 +226,22 @@
     inside = pl.BlockSpec(memory_space=pltpu.VMEM)
     return pl.pallas_call(
         functools.partial(gradient_kernel, factor),
-        in_specs=[anywhere, anywhere, anywhere, inside, inside],
+        in_specs=[anywhere, anywhere, inside, inside, inside],
         out_specs=inside,
         out_shape=jax.ShapeDtypeStruct((2, width + harmonics + LANES), jnp.float32),
         scratch_shapes=[
             pltpu.VMEM((2, harmonics, owned), jnp.bfloat16),
-            pltpu.VMEM((2, owned), jnp.float32),
             pltpu.VMEM((2, harmonics), jnp.float32),
         ]
-        + [table] * 8
-        + [column] * 4
+        + [table] * 11
+        + [column] * 5
         + [
             pltpu.VMEM((GROUP, LANES), jnp.float32),
             pltpu.SemaphoreType.DMA((harmonics // ROWS,)),
-            pltpu.SemaphoreType.DMA((2,)),
+            pltpu.SemaphoreType.DMA,
         ],
         compiler_params=pltpu.CompilerParams(vmem_limit_bytes=VMEM_LIMIT),
-    )(*(pltpu.with_memory_space_constraint(x, pltpu.HBM) for x in (spectra, own, prof)), prev, after)
+    )(*(pltpu.with_memory_space_constraint(x, pltpu.HBM) for x in (spectra, prof)), own, prev, after)
 
 
 def final_kernel(weight, sums, grads, low_add, high_add, filt, prof, filt_out, prof_out, misfit):
@@ -303,7 +332,9 @@
     width = owned + 2 * harmonics
     weight = 1.0 / (lax.axis_size("sub") * spectra.shape[0] * harmonics)
     prev, after = neighbours(filter_init, filter_init, "chan")
-    local = local_gradients(-2.0 * weight, spectra, filter_init, profile_init, prev, after)
+    scale = jnp.where(lax.axis_index("chan") >= 0, 1.0, 0.0).astype(jnp.float32)
+    own = filter_init * scale
+    local = local_gradients(-2.0 * weight, spectra, own, profile_init, prev, after)
     for mask in (2, 6, 1):
         local = local + swap(local, "sub", mask)
     grads = local[:, :width]

time: 50.7 us -> 47.5 us (0.937)
  Pallas kernels: 14.8 us -> 11.5 us
  other arithmetic: 0.29 us -> 1.05 us
  waiting for transfers between devices: 19.4 us -> 18.7 us
    pallas_call x1, Pallas kernels: 14 us -> 10.8 us  [local_gradients(): pl.pallas_call(functools.partial(gradient_kernel, factor), in_specs=[anyw...]
    ppermute x1, waiting for transfers between devices: 1.55 us -> 0.79 us  [neighbours(): lax.ppermute(to_next, axis, ahead)]
    mul x0 -> x1, other arithmetic: none -> 0.76 us  [on_device(): own = filter_init * scale]
  transfers between devices with their start and end apart: 9 -> 9, of which waited for: 9 -> 9; matrix products, arithmetic and copies ran while one was open for 0% -> 2% of each run, Pallas kernels for 0% -> 0%
where the time goes in v3:
time: 47.5 us; the launch traced here: 47.3 us
  waiting for transfers between devices  18.7 us (39%)
  starting transfers between devices  15.2 us (32%)
  Pallas kernels  11.5 us (24%)
  other arithmetic  1.05 us (2%)
  between operations  0.83 us (2%)
    ppermute x7, waiting for transfers between devices, swap(): return lax.ppermute(values, axis, [(i, i ^ mask) for i in range(count)])  17.8 us
    ppermute x7, starting transfers between devices, swap(): return lax.ppermute(values, axis, [(i, i ^ mask) for i in range(count)])  11.2 us
    pallas_call x1, Pallas kernels, local_gradients(): pl.pallas_call(functools.partial(gradient_kernel, factor), in_specs=[anyw...  10.8 us
    ppermute x1, starting transfers between devices, neighbours(): lax.ppermute(to_previous, axis, back)  3.96 us
  transfers between devices with their start and end apart: 9, of which 9 were waited for; matrix products, arithmetic and copies ran while one was open for 2% of the time, Pallas kernels for 0%

profile of v3, /device:TPU:0, one launch (start us, length us, event | category | flops | bytes accessed | tf_op | source)
XLA Modules:
  0.0 47.3 jit_solution(15911638136517008103)
XLA Ops:
  0.6 0.0 copy-start
  0.6 0.0 copy-start.1
  0.7 0.1 collective-permute-start
  0.7 4.0 %collective-permute-start.1 = (f32[2,2048]{1,0:T(2,128)}, f32[2,2048]{1,0:T(2,128)S(1)}, u32[]{:S(2)}, u32[]{:S(2)}) collective-permute-start(f32[2,2048]{1,0:T(2,128)} %filt.1), channel_id=1, source_target_pairs={{8,0},{16,8},{24,16},{32,24},{40,32},{48,40},{56,48},{64,56},{72,6... | collective-permute-start | bytes 49160 | tf_op jit(solution)/shard_map/ppermute | solution.py:299
  4.7 0.8 %broadcast_multiply_fusion.own = f32[2,2048]{1,0:T(2,128)S(1)} fusion(f32[2,2048]{1,0:T(2,128)} %filt.1, f32[]{:T(128)S(6)} %select_n.114), kind=kLoop, calls=%fused_computation.10 | loop fusion | flops 4096 | bytes 32772 | tf_op jit(solution)/shard_map/mul | solution.py:336
  5.5 0.8 %collective-permute-done.prev = f32[2,2048]{1,0:T(2,128)S(1)} collective-permute-done((f32[2,2048]{1,0:T(2,128)}, f32[2,2048]{1,0:T(2,128)S(1)}, u32[]{:S(2)}, u32[]{:S(2)}) %collective-permute-start) | collective-permute-done | bytes 16416 | tf_op jit(solution)/shard_map/ppermute | solution.py:299
  6.2 0.1 collective-permute-done.1.after
  6.3 10.8 %shard_map.58 = f32[2,3712]{1,0:T(2,128)S(1)} custom-call(bf16[1,2,512,2048]{3,2,1,0:T(8,128)(2,1)} %spectra.1, f32[2,512]{1,0:T(2,128)} %prof.1, f32[2,2048]{1,0:T(2,128)S(1)} %broadcast_multiply_fusion.own, f32[2,2048]{1,0:T(2,128)S(1)} %collective-permute-done.prev, f32[2,2048]{1,0:T(2,128)S(1)} %collective-permute-done.1.after), custom_call_target="tpu_custom_call" | custom-call | tf_op jit(solution)/shard_map/pallas_call | solution.py:227
  17.1 1.6 %collective-permute-start.2 = (f32[2,3712]{1,0:T(2,128)S(1)}, f32[2,3712]{1,0:T(2,128)S(1)}, u32[]{:S(2)}, u32[]{:S(2)}) collective-permute-start(f32[2,3712]{1,0:T(2,128)S(1)} %shard_map.58), channel_id=1, source_target_pairs={{0,2},{1,3},{2,0},{3,1},{4,6},{5,7},{6,4},{7,5},{8,10},{9,11},{10,... | collective-permute-start | bytes 89096 | tf_op jit(solution)/shard_map/ppermute | solution.py:292
  18.7 2.4 %collective-permute-done.2 = f32[2,3712]{1,0:T(2,128)S(1)} collective-permute-done((f32[2,3712]{1,0:T(2,128)S(1)}, f32[2,3712]{1,0:T(2,128)S(1)}, u32[]{:S(2)}, u32[]{:S(2)}) %collective-permute-start.2) | collective-permute-done | bytes 29728 | tf_op jit(solution)/shard_map/ppermute | solution.py:292
  21.1 2.8 %collective-permute-start.3 = (f32[2,3712]{1,0:T(2,128)S(1)}, f32[2,3712]{1,0:T(2,128)S(1)}, u32[]{:S(2)}, u32[]{:S(2)}) collective-permute-start(f32[2,3712]{1,0:T(2,128)S(1)} %add.186), channel_id=1, source_target_pairs={{0,6},{1,7},{2,4},{3,5},{4,2},{5,3},{6,0},{7,1},{8,14},{9,15},{10,... | collective-permute-start | bytes 89096 | tf_op jit(solution)/shard_map/ppermute | solution.py:292
  23.9 2.3 %collective-permute-done.3 = f32[2,3712]{1,0:T(2,128)S(1)} collective-permute-done((f32[2,3712]{1,0:T(2,128)S(1)}, f32[2,3712]{1,0:T(2,128)S(1)}, u32[]{:S(2)}, u32[]{:S(2)}) %collective-permute-start.3) | collective-permute-done | bytes 29728 | tf_op jit(solution)/shard_map/ppermute | solution.py:292
  26.3 3.9 %collective-permute-start.4 = (f32[2,3712]{1,0:T(2,128)S(1)}, f32[2,3712]{1,0:T(2,128)S(1)}, u32[]{:S(2)}, u32[]{:S(2)}) collective-permute-start(f32[2,3712]{1,0:T(2,128)S(1)} %add.187), channel_id=1, source_target_pairs={{0,1},{1,0},{2,3},{3,2},{4,5},{5,4},{6,7},{7,6},{8,9},{9,8},{10,11... | collective-permute-start | bytes 89096 | tf_op jit(solution)/shard_map/ppermute | solution.py:292
  30.2 1.9 %collective-permute-done.4 = f32[2,3712]{1,0:T(2,128)S(1)} collective-permute-done((f32[2,3712]{1,0:T(2,128)S(1)}, f32[2,3712]{1,0:T(2,128)S(1)}, u32[]{:S(2)}, u32[]{:S(2)}) %collective-permute-start.4) | collective-permute-done | bytes 29728 | tf_op jit(solution)/shard_map/ppermute | solution.py:292
  32.2 0.1 collective-permute-start.5
  32.3 1.2 %collective-permute-done.5 = f32[2,2816]{1,0:T(2,128)S(1)} collective-permute-done((f32[2,2816]{1,0:T(2,128)S(1)}, f32[2,2816]{1,0:T(2,128)S(1)}, u32[]{:S(2)}, u32[]{:S(2)}) %collective-permute-start.5) | collective-permute-done | bytes 22560 | tf_op jit(solution)/shard_map/ppermute | solution.py:292
  33.5 0.1 collective-permute-start.6
  33.6 3.8 %collective-permute-done.6 = f32[2,2816]{1,0:T(2,128)S(1)} collective-permute-done((f32[2,2816]{1,0:T(2,128)S(1)}, f32[2,2816]{1,0:T(2,128)S(1)}, u32[]{:S(2)}, u32[]{:S(2)}) %collective-permute-start.6) | collective-permute-done | bytes 22560 | tf_op jit(solution)/shard_map/ppermute | solution.py:292
  37.5 0.6 %collective-permute-start.7 = (f32[2,2816]{1,0:T(2,128)S(1)}, f32[2,2816]{1,0:T(2,128)S(1)}, u32[]{:S(2)}, u32[]{:S(2)}) collective-permute-start(f32[2,2816]{1,0:T(2,128)S(1)} %pad_maximum_fusion.2), channel_id=1, source_target_pairs={{0,32},{8,40},{16,48},{24,56},{32,0},{40,8},{48,16},{56,24},{64,96... | collective-permute-start | bytes 67592 | tf_op jit(solution)/shard_map/ppermute | solution.py:292
  38.1 3.3 %collective-permute-done.7 = f32[2,2816]{1,0:T(2,128)S(1)} collective-permute-done((f32[2,2816]{1,0:T(2,128)S(1)}, f32[2,2816]{1,0:T(2,128)S(1)}, u32[]{:S(2)}, u32[]{:S(2)}) %collective-permute-start.7) | collective-permute-done | bytes 22560 | tf_op jit(solution)/shard_map/ppermute | solution.py:292
  41.4 2.0 %collective-permute-start.8 = (f32[2,1792]{1,0:T(2,128)S(1)}, f32[2,1792]{1,0:T(2,128)S(1)}, u32[]{:S(2)}, u32[]{:S(2)}) collective-permute-start(f32[2,1792]{1,0:T(2,128)S(1)} %pad_maximum_fusion.3), channel_id=1, source_target_pairs={{0,96},{8,104},{16,112},{24,120},{32,64},{40,72},{48,80},{56,88},{... | collective-permute-start | bytes 43016 | tf_op jit(solution)/shard_map/ppermute | solution.py:292
  43.5 3.0 %collective-permute-done.8 = f32[2,1792]{1,0:T(2,128)S(1)} collective-permute-done((f32[2,1792]{1,0:T(2,128)S(1)}, f32[2,1792]{1,0:T(2,128)S(1)}, u32[]{:S(2)}, u32[]{:S(2)}) %collective-permute-start.8) | collective-permute-done | bytes 14368 | tf_op jit(solution)/shard_map/ppermute | solution.py:292
  46.5 0.0 copy-done
  46.5 0.0 copy-done.1
  46.5 0.8 %shard_map.59 = (f32[2,2048]{1,0:T(2,128)}, f32[2,512]{1,0:T(2,128)}, f32[1]{0:T(128)}) custom-call(f32[2,768]{1,0:T(2,128)S(1)} %pad_maximum_fusion.4.sums, f32[2,3072]{1,0:T(2,128)S(1)} %get-tuple-element.15.grads, f32[2,1024]{1,0:T(2,128)S(1)} %get-tuple-element.8.low_add, f32[2,1024]{1,0:T(2,128)S(1)} %get-tuple-element.7.high_add, ...), custom_call_target="tpu_custom_call" | custom-call | tf_op jit(solution)/shard_map/pallas_call | solution.py:270
  (28 shorter events, 0.3 us)
Async XLA Ops:
  0.6 45.9 %copy-start = (f32[2,2048]{1,0:T(2,128)S(1)}, f32[2,2048]{1,0:T(2,128)}, u32[]{:S(2)}) copy-start(f32[2,2048]{1,0:T(2,128)} %filt.1) | copy-start | bytes 49156
  0.6 45.9 %copy-start.1 = (f32[2,512]{1,0:T(2,128)S(1)}, f32[2,512]{1,0:T(2,128)}, u32[]{:S(2)}) copy-start(f32[2,512]{1,0:T(2,128)} %prof.1) | copy-start | bytes 12292
  0.7 5.6 %collective-permute-start = (f32[2,2048]{1,0:T(2,128)}, f32[2,2048]{1,0:T(2,128)S(1)}, u32[]{:S(2)}, u32[]{:S(2)}) collective-permute-start(f32[2,2048]{1,0:T(2,128)} %filt.1), channel_id=1, source_target_pairs={{0,8},{8,16},{16,24},{24,32},{32,40},{40,48},{48,56},{56,64},{64,7... | collective-permute-start | bytes 49160 | tf_op jit(solution)/shard_map/ppermute | solution.py:299
  0.7 5.6 %collective-permute-start.1 = (f32[2,2048]{1,0:T(2,128)}, f32[2,2048]{1,0:T(2,128)S(1)}, u32[]{:S(2)}, u32[]{:S(2)}) collective-permute-start(f32[2,2048]{1,0:T(2,128)} %filt.1), channel_id=1, source_target_pairs={{8,0},{16,8},{24,16},{32,24},{40,32},{48,40},{56,48},{64,56},{72,6... | collective-permute-start | bytes 49160 | tf_op jit(solution)/shard_map/ppermute | solution.py:299
  17.1 4.0 %collective-permute-start.2 = (f32[2,3712]{1,0:T(2,128)S(1)}, f32[2,3712]{1,0:T(2,128)S(1)}, u32[]{:S(2)}, u32[]{:S(2)}) collective-permute-start(f32[2,3712]{1,0:T(2,128)S(1)} %shard_map.58), channel_id=1, source_target_pairs={{0,2},{1,3},{2,0},{3,1},{4,6},{5,7},{6,4},{7,5},{8,10},{9,11},{10,... | collective-permute-start | bytes 89096 | tf_op jit(solution)/shard_map/ppermute | solution.py:292
  21.1 5.2 %collective-permute-start.3 = (f32[2,3712]{1,0:T(2,128)S(1)}, f32[2,3712]{1,0:T(2,128)S(1)}, u32[]{:S(2)}, u32[]{:S(2)}) collective-permute-start(f32[2,3712]{1,0:T(2,128)S(1)} %add.186), channel_id=1, source_target_pairs={{0,6},{1,7},{2,4},{3,5},{4,2},{5,3},{6,0},{7,1},{8,14},{9,15},{10,... | collective-permute-start | bytes 89096 | tf_op jit(solution)/shard_map/ppermute | solution.py:292
  26.3 5.8 %collective-permute-start.4 = (f32[2,3712]{1,0:T(2,128)S(1)}, f32[2,3712]{1,0:T(2,128)S(1)}, u32[]{:S(2)}, u32[]{:S(2)}) collective-permute-start(f32[2,3712]{1,0:T(2,128)S(1)} %add.187), channel_id=1, source_target_pairs={{0,1},{1,0},{2,3},{3,2},{4,5},{5,4},{6,7},{7,6},{8,9},{9,8},{10,11... | collective-permute-start | bytes 89096 | tf_op jit(solution)/shard_map/ppermute | solution.py:292
  32.2 1.3 %collective-permute-start.5 = (f32[2,2816]{1,0:T(2,128)S(1)}, f32[2,2816]{1,0:T(2,128)S(1)}, u32[]{:S(2)}, u32[]{:S(2)}) collective-permute-start(f32[2,2816]{1,0:T(2,128)S(1)} %pad_maximum_fusion), channel_id=1, source_target_pairs={{0,8},{8,0},{16,24},{24,16},{32,40},{40,32},{48,56},{56,48},{64,72... | collective-permute-start | bytes 67592 | tf_op jit(solution)/shard_map/ppermute | solution.py:292
  33.5 3.9 %collective-permute-start.6 = (f32[2,2816]{1,0:T(2,128)S(1)}, f32[2,2816]{1,0:T(2,128)S(1)}, u32[]{:S(2)}, u32[]{:S(2)}) collective-permute-start(f32[2,2816]{1,0:T(2,128)S(1)} %pad_maximum_fusion.1), channel_id=1, source_target_pairs={{0,16},{8,24},{16,0},{24,8},{32,48},{40,56},{48,32},{56,40},{64,80... | collective-permute-start | bytes 67592 | tf_op jit(solution)/shard_map/ppermute | solution.py:292
  37.5 3.9 %collective-permute-start.7 = (f32[2,2816]{1,0:T(2,128)S(1)}, f32[2,2816]{1,0:T(2,128)S(1)}, u32[]{:S(2)}, u32[]{:S(2)}) collective-permute-start(f32[2,2816]{1,0:T(2,128)S(1)} %pad_maximum_fusion.2), channel_id=1, source_target_pairs={{0,32},{8,40},{16,48},{24,56},{32,0},{40,8},{48,16},{56,24},{64,96... | collective-permute-start | bytes 67592 | tf_op jit(solution)/shard_map/ppermute | solution.py:292
  41.4 5.0 %collective-permute-start.8 = (f32[2,1792]{1,0:T(2,128)S(1)}, f32[2,1792]{1,0:T(2,128)S(1)}, u32[]{:S(2)}, u32[]{:S(2)}) collective-permute-start(f32[2,1792]{1,0:T(2,128)S(1)} %pad_maximum_fusion.3), channel_id=1, source_target_pairs={{0,96},{8,104},{16,112},{24,120},{32,64},{40,72},{48,80},{56,88},{... | collective-permute-start | bytes 43016 | tf_op jit(solution)/shard_map/ppermute | solution.py:292

commit v4 on v3

--- a/solution.py
+++ b/solution.py
@@ -11,7 +11,7 @@
 LANES = 128
 ROWS = 128
 GROUP = 16
-UNROLL = 2
+UNROLL = 8
 VMEM_LIMIT = 28 * 1024 * 1024
 
 filter_rate = 0.1
@@ -29,10 +29,10 @@
 
 
 def gradient_kernel(
-    factor, spectra, prof_hbm, own, prev, after, out,
-    data, prof, fwd_re, fwd_im, fwd_sum, fwd_dif, bwd_re, bwd_sum, bwd_dif,
+    factor, spectra, prof, own, prev, after, out,
+    data, fwd_re, fwd_im, fwd_sum, fwd_dif, bwd_re, bwd_sum, bwd_dif,
     up_re, up_im, down_re, down_im,
-    unit_re, unit_im, size, part_re, part_im, err, block_sems, prof_sem,
+    unit_re, unit_im, size, part_re, part_im, err, block_sems,
 ):
     owned = own.shape[1]
     harmonics = prof.shape[1]
@@ -51,8 +51,6 @@
         )
         for q in range(blocks)
     ]
-    prof_copy = pltpu.make_async_copy(prof_hbm, prof, prof_sem)
-    prof_copy.start()
     for copy in copies:
         copy.start()
 
@@ -94,7 +92,6 @@
         fwd_sum[rows, ahead] = re + im
         fwd_dif[rows, ahead] = re - im
 
-    prof_copy.wait()
     prof_re = prof[0:1, :]
     prof_im = prof[1:2, :]
     length = jnp.sqrt(prof_re * prof_re + prof_im * prof_im)
@@ -226,22 +223,20 @@
     inside = pl.BlockSpec(memory_space=pltpu.VMEM)
     return pl.pallas_call(
         functools.partial(gradient_kernel, factor),
-        in_specs=[anywhere, anywhere, inside, inside, inside],
+        in_specs=[anywhere, inside, inside, inside, inside],
         out_specs=inside,
         out_shape=jax.ShapeDtypeStruct((2, width + harmonics + LANES), jnp.float32),
         scratch_shapes=[
             pltpu.VMEM((2, harmonics, owned), jnp.bfloat16),
-            pltpu.VMEM((2, harmonics), jnp.float32),
         ]
         + [table] * 11
         + [column] * 5
         + [
             pltpu.VMEM((GROUP, LANES), jnp.float32),
             pltpu.SemaphoreType.DMA((harmonics // ROWS,)),
-            pltpu.SemaphoreType.DMA,
         ],
         compiler_params=pltpu.CompilerParams(vmem_limit_bytes=VMEM_LIMIT),
-    )(*(pltpu.with_memory_space_constraint(x, pltpu.HBM) for x in (spectra, prof)), own, prev, after)
+    )(pltpu.with_memory_space_constraint(spectra, pltpu.HBM), prof, own, prev, after)
 
 
 def final_kernel(weight, sums, grads, low_add, high_add, filt, prof, filt_out, prof_out, misfit):
@@ -334,7 +329,7 @@
     prev, after = neighbours(filter_init, filter_init, "chan")
     scale = jnp.where(lax.axis_index("chan") >= 0, 1.0, 0.0).astype(jnp.float32)
     own = filter_init * scale
-    local = local_gradients(-2.0 * weight, spectra, own, profile_init, prev, after)
+    local = local_gradients(-2.0 * weight, spectra, own, profile_init * scale, prev, after)
     for mask in (2, 6, 1):
         local = local + swap(local, "sub", mask)
     grads = local[:, :width]

time: 47.5 us -> 46.6 us (0.981)
  Pallas kernels: 11.5 us -> 10.6 us
  waiting for transfers between devices: 18.7 us -> 18 us
  other arithmetic: 1.05 us -> 1.74 us
    pallas_call x1, Pallas kernels: 10.8 us -> 9.86 us  [local_gradients(): pl.pallas_call(functools.partial(gradient_kernel, factor), in_specs=[anyw...]
    ppermute x1, waiting for transfers between devices: 0.79 us -> 0.1 us  [neighbours(): lax.ppermute(to_next, axis, ahead)]
    mul x0 -> x1, other arithmetic: none -> 0.69 us  [on_device(): profile_init * scale]
  transfers between devices with their start and end apart: 9 -> 9, of which waited for: 9 -> 9; matrix products, arithmetic and copies ran while one was open for 2% -> 3% of each run, Pallas kernels for 0% -> 0%
where the time goes in v4:
time: 46.6 us; the launch traced here: 46.4 us
  waiting for transfers between devices  18 us (39%)
  starting transfers between devices  15.2 us (33%)
  Pallas kernels  10.6 us (23%)
  other arithmetic  1.74 us (4%)
  between operations  0.83 us (2%)
    ppermute x7, waiting for transfers between devices, swap(): return lax.ppermute(values, axis, [(i, i ^ mask) for i in range(count)])  17.8 us
    ppermute x7, starting transfers between devices, swap(): return lax.ppermute(values, axis, [(i, i ^ mask) for i in range(count)])  11.2 us
    pallas_call x1, Pallas kernels, local_gradients(): pl.pallas_call(functools.partial(gradient_kernel, factor), in_specs=[anyw...  9.86 us
    ppermute x1, starting transfers between devices, neighbours(): lax.ppermute(to_previous, axis, back)  3.96 us
  transfers between devices with their start and end apart: 9, of which 9 were waited for; matrix products, arithmetic and copies ran while one was open for 3% of the time, Pallas kernels for 0%

profile of v4, /device:TPU:0, one launch (start us, length us, event | category | flops | bytes accessed | tf_op | source)
XLA Modules:
  0.0 46.4 jit_solution(8707342522436006730)
XLA Ops:
  0.6 0.0 copy-start
  0.6 0.0 copy-start.1
  0.7 0.1 collective-permute-start
  0.7 4.0 %collective-permute-start.1 = (f32[2,2048]{1,0:T(2,128)}, f32[2,2048]{1,0:T(2,128)S(1)}, u32[]{:S(2)}, u32[]{:S(2)}) collective-permute-start(f32[2,2048]{1,0:T(2,128)} %filt.1), channel_id=1, source_target_pairs={{8,0},{16,8},{24,16},{32,24},{40,32},{48,40},{56,48},{64,56},{72,6... | collective-permute-start | bytes 49160 | tf_op jit(solution)/shard_map/ppermute | solution.py:294
  4.7 0.8 %broadcast_multiply_fusion.own = f32[2,2048]{1,0:T(2,128)S(1)} fusion(f32[2,2048]{1,0:T(2,128)} %filt.1, f32[]{:T(128)S(6)} %select_n.114), kind=kLoop, calls=%fused_computation.10 | loop fusion | flops 4096 | bytes 32772 | tf_op jit(solution)/shard_map/mul | solution.py:331
  5.5 0.7 %broadcast_multiply_fusion.1.prof = f32[2,512]{1,0:T(2,128)S(1)} fusion(f32[2,512]{1,0:T(2,128)} %prof.1, f32[]{:T(128)S(6)} %select_n.114), kind=kLoop, calls=%fused_computation.24 | loop fusion | flops 1024 | bytes 8196 | tf_op jit(solution)/shard_map/mul | solution.py:332
  6.1 0.1 collective-permute-done.prev
  6.2 0.1 collective-permute-done.1.after
  6.3 9.9 %shard_map.58 = f32[2,3712]{1,0:T(2,128)S(1)} custom-call(bf16[1,2,512,2048]{3,2,1,0:T(8,128)(2,1)} %spectra.1, f32[2,512]{1,0:T(2,128)S(1)} %broadcast_multiply_fusion.1.prof, f32[2,2048]{1,0:T(2,128)S(1)} %broadcast_multiply_fusion.own, f32[2,2048]{1,0:T(2,128)S(1)} %collective-permute-done.prev, f32[2,2048]{1,0:T(2,128)S(1)} %collective-permute-done.1.after), custom_call_target="tpu_custom_call" | custom-call | tf_op jit(solution)/shard_map/pallas_call | solution.py:224
  16.2 1.6 %collective-permute-start.2 = (f32[2,3712]{1,0:T(2,128)S(1)}, f32[2,3712]{1,0:T(2,128)S(1)}, u32[]{:S(2)}, u32[]{:S(2)}) collective-permute-start(f32[2,3712]{1,0:T(2,128)S(1)} %shard_map.58), channel_id=1, source_target_pairs={{0,2},{1,3},{2,0},{3,1},{4,6},{5,7},{6,4},{7,5},{8,10},{9,11},{10,... | collective-permute-start | bytes 89096 | tf_op jit(solution)/shard_map/ppermute | solution.py:287
  17.8 2.4 %collective-permute-done.2 = f32[2,3712]{1,0:T(2,128)S(1)} collective-permute-done((f32[2,3712]{1,0:T(2,128)S(1)}, f32[2,3712]{1,0:T(2,128)S(1)}, u32[]{:S(2)}, u32[]{:S(2)}) %collective-permute-start.2) | collective-permute-done | bytes 29728 | tf_op jit(solution)/shard_map/ppermute | solution.py:287
  20.2 2.8 %collective-permute-start.3 = (f32[2,3712]{1,0:T(2,128)S(1)}, f32[2,3712]{1,0:T(2,128)S(1)}, u32[]{:S(2)}, u32[]{:S(2)}) collective-permute-start(f32[2,3712]{1,0:T(2,128)S(1)} %add.186), channel_id=1, source_target_pairs={{0,6},{1,7},{2,4},{3,5},{4,2},{5,3},{6,0},{7,1},{8,14},{9,15},{10,... | collective-permute-start | bytes 89096 | tf_op jit(solution)/shard_map/ppermute | solution.py:287
  23.0 2.3 %collective-permute-done.3 = f32[2,3712]{1,0:T(2,128)S(1)} collective-permute-done((f32[2,3712]{1,0:T(2,128)S(1)}, f32[2,3712]{1,0:T(2,128)S(1)}, u32[]{:S(2)}, u32[]{:S(2)}) %collective-permute-start.3) | collective-permute-done | bytes 29728 | tf_op jit(solution)/shard_map/ppermute | solution.py:287
  25.4 3.9 %collective-permute-start.4 = (f32[2,3712]{1,0:T(2,128)S(1)}, f32[2,3712]{1,0:T(2,128)S(1)}, u32[]{:S(2)}, u32[]{:S(2)}) collective-permute-start(f32[2,3712]{1,0:T(2,128)S(1)} %add.187), channel_id=1, source_target_pairs={{0,1},{1,0},{2,3},{3,2},{4,5},{5,4},{6,7},{7,6},{8,9},{9,8},{10,11... | collective-permute-start | bytes 89096 | tf_op jit(solution)/shard_map/ppermute | solution.py:287
  29.3 1.9 %collective-permute-done.4 = f32[2,3712]{1,0:T(2,128)S(1)} collective-permute-done((f32[2,3712]{1,0:T(2,128)S(1)}, f32[2,3712]{1,0:T(2,128)S(1)}, u32[]{:S(2)}, u32[]{:S(2)}) %collective-permute-start.4) | collective-permute-done | bytes 29728 | tf_op jit(solution)/shard_map/ppermute | solution.py:287
  31.3 0.1 collective-permute-start.5
  31.4 1.2 %collective-permute-done.5 = f32[2,2816]{1,0:T(2,128)S(1)} collective-permute-done((f32[2,2816]{1,0:T(2,128)S(1)}, f32[2,2816]{1,0:T(2,128)S(1)}, u32[]{:S(2)}, u32[]{:S(2)}) %collective-permute-start.5) | collective-permute-done | bytes 22560 | tf_op jit(solution)/shard_map/ppermute | solution.py:287
  32.6 0.1 collective-permute-start.6
  32.7 3.8 %collective-permute-done.6 = f32[2,2816]{1,0:T(2,128)S(1)} collective-permute-done((f32[2,2816]{1,0:T(2,128)S(1)}, f32[2,2816]{1,0:T(2,128)S(1)}, u32[]{:S(2)}, u32[]{:S(2)}) %collective-permute-start.6) | collective-permute-done | bytes 22560 | tf_op jit(solution)/shard_map/ppermute | solution.py:287
  36.6 0.6 %collective-permute-start.7 = (f32[2,2816]{1,0:T(2,128)S(1)}, f32[2,2816]{1,0:T(2,128)S(1)}, u32[]{:S(2)}, u32[]{:S(2)}) collective-permute-start(f32[2,2816]{1,0:T(2,128)S(1)} %pad_maximum_fusion.2), channel_id=1, source_target_pairs={{0,32},{8,40},{16,48},{24,56},{32,0},{40,8},{48,16},{56,24},{64,96... | collective-permute-start | bytes 67592 | tf_op jit(solution)/shard_map/ppermute | solution.py:287
  37.2 3.3 %collective-permute-done.7 = f32[2,2816]{1,0:T(2,128)S(1)} collective-permute-done((f32[2,2816]{1,0:T(2,128)S(1)}, f32[2,2816]{1,0:T(2,128)S(1)}, u32[]{:S(2)}, u32[]{:S(2)}) %collective-permute-start.7) | collective-permute-done | bytes 22560 | tf_op jit(solution)/shard_map/ppermute | solution.py:287
  40.5 2.0 %collective-permute-start.8 = (f32[2,1792]{1,0:T(2,128)S(1)}, f32[2,1792]{1,0:T(2,128)S(1)}, u32[]{:S(2)}, u32[]{:S(2)}) collective-permute-start(f32[2,1792]{1,0:T(2,128)S(1)} %pad_maximum_fusion.3), channel_id=1, source_target_pairs={{0,96},{8,104},{16,112},{24,120},{32,64},{40,72},{48,80},{56,88},{... | collective-permute-start | bytes 43016 | tf_op jit(solution)/shard_map/ppermute | solution.py:287
  42.6 3.0 %collective-permute-done.8 = f32[2,1792]{1,0:T(2,128)S(1)} collective-permute-done((f32[2,1792]{1,0:T(2,128)S(1)}, f32[2,1792]{1,0:T(2,128)S(1)}, u32[]{:S(2)}, u32[]{:S(2)}) %collective-permute-start.8) | collective-permute-done | bytes 14368 | tf_op jit(solution)/shard_map/ppermute | solution.py:287
  45.6 0.0 copy-done
  45.6 0.0 copy-done.1
  45.6 0.8 %shard_map.59 = (f32[2,2048]{1,0:T(2,128)}, f32[2,512]{1,0:T(2,128)}, f32[1]{0:T(128)}) custom-call(f32[2,768]{1,0:T(2,128)S(1)} %pad_maximum_fusion.4.sums, f32[2,3072]{1,0:T(2,128)S(1)} %get-tuple-element.15.grads, f32[2,1024]{1,0:T(2,128)S(1)} %get-tuple-element.8.low_add, f32[2,1024]{1,0:T(2,128)S(1)} %get-tuple-element.7.high_add, ...), custom_call_target="tpu_custom_call" | custom-call | tf_op jit(solution)/shard_map/pallas_call | solution.py:265
  (28 shorter events, 0.3 us)
Async XLA Ops:
  0.6 45.0 %copy-start = (f32[2,2048]{1,0:T(2,128)S(1)}, f32[2,2048]{1,0:T(2,128)}, u32[]{:S(2)}) copy-start(f32[2,2048]{1,0:T(2,128)} %filt.1) | copy-start | bytes 49156
  0.6 45.0 %copy-start.1 = (f32[2,512]{1,0:T(2,128)S(1)}, f32[2,512]{1,0:T(2,128)}, u32[]{:S(2)}) copy-start(f32[2,512]{1,0:T(2,128)} %prof.1) | copy-start | bytes 12292
  0.7 5.6 %collective-permute-start = (f32[2,2048]{1,0:T(2,128)}, f32[2,2048]{1,0:T(2,128)S(1)}, u32[]{:S(2)}, u32[]{:S(2)}) collective-permute-start(f32[2,2048]{1,0:T(2,128)} %filt.1), channel_id=1, source_target_pairs={{0,8},{8,16},{16,24},{24,32},{32,40},{40,48},{48,56},{56,64},{64,7... | collective-permute-start | bytes 49160 | tf_op jit(solution)/shard_map/ppermute | solution.py:294
  0.7 5.6 %collective-permute-start.1 = (f32[2,2048]{1,0:T(2,128)}, f32[2,2048]{1,0:T(2,128)S(1)}, u32[]{:S(2)}, u32[]{:S(2)}) collective-permute-start(f32[2,2048]{1,0:T(2,128)} %filt.1), channel_id=1, source_target_pairs={{8,0},{16,8},{24,16},{32,24},{40,32},{48,40},{56,48},{64,56},{72,6... | collective-permute-start | bytes 49160 | tf_op jit(solution)/shard_map/ppermute | solution.py:294
  16.2 4.0 %collective-permute-start.2 = (f32[2,3712]{1,0:T(2,128)S(1)}, f32[2,3712]{1,0:T(2,128)S(1)}, u32[]{:S(2)}, u32[]{:S(2)}) collective-permute-start(f32[2,3712]{1,0:T(2,128)S(1)} %shard_map.58), channel_id=1, source_target_pairs={{0,2},{1,3},{2,0},{3,1},{4,6},{5,7},{6,4},{7,5},{8,10},{9,11},{10,... | collective-permute-start | bytes 89096 | tf_op jit(solution)/shard_map/ppermute | solution.py:287
  20.2 5.2 %collective-permute-start.3 = (f32[2,3712]{1,0:T(2,128)S(1)}, f32[2,3712]{1,0:T(2,128)S(1)}, u32[]{:S(2)}, u32[]{:S(2)}) collective-permute-start(f32[2,3712]{1,0:T(2,128)S(1)} %add.186), channel_id=1, source_target_pairs={{0,6},{1,7},{2,4},{3,5},{4,2},{5,3},{6,0},{7,1},{8,14},{9,15},{10,... | collective-permute-start | bytes 89096 | tf_op jit(solution)/shard_map/ppermute | solution.py:287
  25.4 5.8 %collective-permute-start.4 = (f32[2,3712]{1,0:T(2,128)S(1)}, f32[2,3712]{1,0:T(2,128)S(1)}, u32[]{:S(2)}, u32[]{:S(2)}) collective-permute-start(f32[2,3712]{1,0:T(2,128)S(1)} %add.187), channel_id=1, source_target_pairs={{0,1},{1,0},{2,3},{3,2},{4,5},{5,4},{6,7},{7,6},{8,9},{9,8},{10,11... | collective-permute-start | bytes 89096 | tf_op jit(solution)/shard_map/ppermute | solution.py:287
  31.3 1.3 %collective-permute-start.5 = (f32[2,2816]{1,0:T(2,128)S(1)}, f32[2,2816]{1,0:T(2,128)S(1)}, u32[]{:S(2)}, u32[]{:S(2)}) collective-permute-start(f32[2,2816]{1,0:T(2,128)S(1)} %pad_maximum_fusion), channel_id=1, source_target_pairs={{0,8},{8,0},{16,24},{24,16},{32,40},{40,32},{48,56},{56,48},{64,72... | collective-permute-start | bytes 67592 | tf_op jit(solution)/shard_map/ppermute | solution.py:287
  32.6 3.9 %collective-permute-start.6 = (f32[2,2816]{1,0:T(2,128)S(1)}, f32[2,2816]{1,0:T(2,128)S(1)}, u32[]{:S(2)}, u32[]{:S(2)}) collective-permute-start(f32[2,2816]{1,0:T(2,128)S(1)} %pad_maximum_fusion.1), channel_id=1, source_target_pairs={{0,16},{8,24},{16,0},{24,8},{32,48},{40,56},{48,32},{56,40},{64,80... | collective-permute-start | bytes 67592 | tf_op jit(solution)/shard_map/ppermute | solution.py:287
  36.6 3.9 %collective-permute-start.7 = (f32[2,2816]{1,0:T(2,128)S(1)}, f32[2,2816]{1,0:T(2,128)S(1)}, u32[]{:S(2)}, u32[]{:S(2)}) collective-permute-start(f32[2,2816]{1,0:T(2,128)S(1)} %pad_maximum_fusion.2), channel_id=1, source_target_pairs={{0,32},{8,40},{16,48},{24,56},{32,0},{40,8},{48,16},{56,24},{64,96... | collective-permute-start | bytes 67592 | tf_op jit(solution)/shard_map/ppermute | solution.py:287
  40.5 5.0 %collective-permute-start.8 = (f32[2,1792]{1,0:T(2,128)S(1)}, f32[2,1792]{1,0:T(2,128)S(1)}, u32[]{:S(2)}, u32[]{:S(2)}) collective-permute-start(f32[2,1792]{1,0:T(2,128)S(1)} %pad_maximum_fusion.3), channel_id=1, source_target_pairs={{0,96},{8,104},{16,112},{24,120},{32,64},{40,72},{48,80},{56,88},{... | collective-permute-start | bytes 43016 | tf_op jit(solution)/shard_map/ppermute | solution.py:287

commit v5 on v4

--- a/solution.py
+++ b/solution.py
@@ -12,7 +12,7 @@
 ROWS = 128
 GROUP = 16
 UNROLL = 8
-VMEM_LIMIT = 28 * 1024 * 1024
+VMEM_LIMIT = 40 * 1024 * 1024
 
 filter_rate = 0.1
 profile_rate = 0.1
@@ -21,6 +21,8 @@
 
 def skew(block, sign):
     width = block.shape[1]
+    if sign > 0 and block.shape[0] == 8:
+        return pltpu.roll(block, 0, 1, stride=1, stride_axis=0)
     row = lax.broadcasted_iota(jnp.int32, block.shape, 0)
     for bit in (1, 2, 4):
         moved = pltpu.roll(block, bit if sign > 0 else width - bit, 1)
@@ -51,8 +53,7 @@
         )
         for q in range(blocks)
     ]
-    for copy in copies:
-        copy.start()
+    copies[0].start()
 
     for acc in (up_re, up_im):
         acc[:, halo - LANES : halo] = jnp.zeros((ROWS, LANES), jnp.float32)
@@ -108,6 +109,9 @@
 
     for q in range(blocks):
         copies[q].wait()
+        if q == 0:
+            for copy in copies[1:]:
+                copy.start()
 
         def group(index, carry, q=q):
             start = pl.multiple_of(index * GROUP, GROUP)
@@ -167,31 +171,32 @@
         lax.fori_loop(0, ROWS // GROUP, group, 0, unroll=UNROLL)
 
     ones = jnp.ones((8, LANES), jnp.float32)
-    span = (owned + halo) // 2
-    raised = []
-    lowered = []
-    for up, down in ((up_re, down_re), (up_im, down_im)):
-        for half in range(2):
-            first = halo - LANES + half * span
-            total = up[0:8, first : first + span + LANES]
-            for a in range(1, ROWS // 8):
-                piece = up[8 * a : 8 * a + 8, first : first + span + LANES]
-                total = total + pltpu.roll(piece, 8 * a, 1)
-            raised.append(total)
-            first = half * span
-            total = down[0:8, first : first + span + LANES]
-            for a in range(1, ROWS // 8):
-                piece = down[8 * a : 8 * a + 8, first : first + span + LANES]
-                total = total + pltpu.roll(piece, span + LANES - 8 * a, 1)
-            lowered.append(total)
-    raised = skew(jnp.concatenate(raised, axis=0), 1)[:, LANES:]
-    lowered = skew(jnp.concatenate(lowered, axis=0), -1)[:, :span]
-    raised = factor * jnp.sum(raised.reshape(4, 8, span), axis=1)
-    lowered = factor * jnp.sum(lowered.reshape(4, 8, span), axis=1)
+    pieces = 4
+    span = (owned + halo) // pieces
+    raised = [[], []]
+    lowered = [[], []]
+    for piece in range(pieces):
+        high = slice(halo - LANES + piece * span, halo + piece * span + span)
+        low = slice(piece * span, piece * span + span + LANES)
+        totals = [jnp.zeros((8, span + LANES), jnp.float32)] * 4
+        for a in range(ROWS // 8):
+            rows = slice(8 * a, 8 * a + 8)
+            back = span + LANES - 8 * a
+            totals[0] = totals[0] + pltpu.roll(up_re[rows, high], 8 * a, 1, stride=1, stride_axis=0)
+            totals[1] = totals[1] + pltpu.roll(up_im[rows, high], 8 * a, 1, stride=1, stride_axis=0)
+            totals[2] = totals[2] + (pltpu.roll(down_re[rows, low], back, 1) if a else down_re[rows, low])
+            totals[3] = totals[3] + (pltpu.roll(down_im[rows, low], back, 1) if a else down_im[rows, low])
+        for part in range(2):
+            raised[part].append(totals[part][:, LANES:])
+            lowered[part].append(totals[2 + part])
+    raised = jnp.concatenate(raised[0] + raised[1], axis=0)
+    lowered = skew(jnp.concatenate(lowered[0] + lowered[1], axis=0), -1)[:, :span]
+    raised = factor * jnp.sum(raised.reshape(2 * pieces, 8, span), axis=1)
+    lowered = factor * jnp.sum(lowered.reshape(2 * pieces, 8, span), axis=1)
     for part in range(2):
         row = slice(part, part + 1)
-        rise = jnp.concatenate([raised[2 * part + i : 2 * part + i + 1] for i in range(2)], axis=1)
-        fall = jnp.concatenate([lowered[2 * part + i : 2 * part + i + 1] for i in range(2)], axis=1)
+        rise = jnp.concatenate([raised[pieces * part + i : pieces * part + i + 1] for i in range(pieces)], axis=1)
+        fall = jnp.concatenate([lowered[pieces * part + i : pieces * part + i + 1] for i in range(pieces)], axis=1)
         out[row, 0:halo] = fall[:, :halo] * keep_low
         out[row, halo : halo + owned] = fall[:, halo:] + rise[:, :owned]
         out[row, halo + owned : width] = rise[:, owned:] * keep_high

time: 46.6 us -> 46.1 us (0.989)
  Pallas kernels: 10.6 us -> 10.1 us
    pallas_call x1, Pallas kernels: 9.86 us -> 9.34 us  [local_gradients(): pl.pallas_call(functools.partial(gradient_kernel, factor), in_specs=[anyw...]
where the time goes in v5:
time: 46.1 us; the launch traced here: 45.9 us
  waiting for transfers between devices  18 us (39%)
  starting transfers between devices  15.2 us (33%)
  Pallas kernels  10.1 us (22%)
  other arithmetic  1.74 us (4%)
  between operations  0.83 us (2%)
    ppermute x7, waiting for transfers between devices, swap(): return lax.ppermute(values, axis, [(i, i ^ mask) for i in range(count)])  17.8 us
    ppermute x7, starting transfers between devices, swap(): return lax.ppermute(values, axis, [(i, i ^ mask) for i in range(count)])  11.2 us
    pallas_call x1, Pallas kernels, local_gradients(): pl.pallas_call(functools.partial(gradient_kernel, factor), in_specs=[anyw...  9.34 us
    ppermute x1, starting transfers between devices, neighbours(): lax.ppermute(to_previous, axis, back)  3.96 us
  transfers between devices with their start and end apart: 9, of which 9 were waited for; matrix products, arithmetic and copies ran while one was open for 3% of the time, Pallas kernels for 0%

profile of v5, /device:TPU:0, one launch (start us, length us, event | category | flops | bytes accessed | tf_op | source)
XLA Modules:
  0.0 45.9 jit_solution(6933586391866492440)
XLA Ops:
  0.6 0.0 copy-start
  0.6 0.0 copy-start.1
  0.7 0.1 collective-permute-start
  0.7 4.0 %collective-permute-start.1 = (f32[2,2048]{1,0:T(2,128)}, f32[2,2048]{1,0:T(2,128)S(1)}, u32[]{:S(2)}, u32[]{:S(2)}) collective-permute-start(f32[2,2048]{1,0:T(2,128)} %filt.1), channel_id=1, source_target_pairs={{8,0},{16,8},{24,16},{32,24},{40,32},{48,40},{56,48},{64,56},{72,6... | collective-permute-start | bytes 49160 | tf_op jit(solution)/shard_map/ppermute | solution.py:299
  4.7 0.8 %broadcast_multiply_fusion.own = f32[2,2048]{1,0:T(2,128)S(1)} fusion(f32[2,2048]{1,0:T(2,128)} %filt.1, f32[]{:T(128)S(6)} %select_n.114), kind=kLoop, calls=%fused_computation.10 | loop fusion | flops 4096 | bytes 32772 | tf_op jit(solution)/shard_map/mul | solution.py:336
  5.5 0.7 %broadcast_multiply_fusion.1.prof = f32[2,512]{1,0:T(2,128)S(1)} fusion(f32[2,512]{1,0:T(2,128)} %prof.1, f32[]{:T(128)S(6)} %select_n.114), kind=kLoop, calls=%fused_computation.24 | loop fusion | flops 1024 | bytes 8196 | tf_op jit(solution)/shard_map/mul | solution.py:337
  6.1 0.1 collective-permute-done.prev
  6.2 0.1 collective-permute-done.1.after
  6.3 9.3 %shard_map.58 = f32[2,3712]{1,0:T(2,128)S(1)} custom-call(bf16[1,2,512,2048]{3,2,1,0:T(8,128)(2,1)} %spectra.1, f32[2,512]{1,0:T(2,128)S(1)} %broadcast_multiply_fusion.1.prof, f32[2,2048]{1,0:T(2,128)S(1)} %broadcast_multiply_fusion.own, f32[2,2048]{1,0:T(2,128)S(1)} %collective-permute-done.prev, f32[2,2048]{1,0:T(2,128)S(1)} %collective-permute-done.1.after), custom_call_target="tpu_custom_call" | custom-call | tf_op jit(solution)/shard_map/pallas_call | solution.py:229
  15.7 1.6 %collective-permute-start.2 = (f32[2,3712]{1,0:T(2,128)S(1)}, f32[2,3712]{1,0:T(2,128)S(1)}, u32[]{:S(2)}, u32[]{:S(2)}) collective-permute-start(f32[2,3712]{1,0:T(2,128)S(1)} %shard_map.58), channel_id=1, source_target_pairs={{0,2},{1,3},{2,0},{3,1},{4,6},{5,7},{6,4},{7,5},{8,10},{9,11},{10,... | collective-permute-start | bytes 89096 | tf_op jit(solution)/shard_map/ppermute | solution.py:292
  17.3 2.4 %collective-permute-done.2 = f32[2,3712]{1,0:T(2,128)S(1)} collective-permute-done((f32[2,3712]{1,0:T(2,128)S(1)}, f32[2,3712]{1,0:T(2,128)S(1)}, u32[]{:S(2)}, u32[]{:S(2)}) %collective-permute-start.2) | collective-permute-done | bytes 29728 | tf_op jit(solution)/shard_map/ppermute | solution.py:292
  19.7 2.8 %collective-permute-start.3 = (f32[2,3712]{1,0:T(2,128)S(1)}, f32[2,3712]{1,0:T(2,128)S(1)}, u32[]{:S(2)}, u32[]{:S(2)}) collective-permute-start(f32[2,3712]{1,0:T(2,128)S(1)} %add.186), channel_id=1, source_target_pairs={{0,6},{1,7},{2,4},{3,5},{4,2},{5,3},{6,0},{7,1},{8,14},{9,15},{10,... | collective-permute-start | bytes 89096 | tf_op jit(solution)/shard_map/ppermute | solution.py:292
  22.5 2.3 %collective-permute-done.3 = f32[2,3712]{1,0:T(2,128)S(1)} collective-permute-done((f32[2,3712]{1,0:T(2,128)S(1)}, f32[2,3712]{1,0:T(2,128)S(1)}, u32[]{:S(2)}, u32[]{:S(2)}) %collective-permute-start.3) | collective-permute-done | bytes 29728 | tf_op jit(solution)/shard_map/ppermute | solution.py:292
  24.9 3.9 %collective-permute-start.4 = (f32[2,3712]{1,0:T(2,128)S(1)}, f32[2,3712]{1,0:T(2,128)S(1)}, u32[]{:S(2)}, u32[]{:S(2)}) collective-permute-start(f32[2,3712]{1,0:T(2,128)S(1)} %add.187), channel_id=1, source_target_pairs={{0,1},{1,0},{2,3},{3,2},{4,5},{5,4},{6,7},{7,6},{8,9},{9,8},{10,11... | collective-permute-start | bytes 89096 | tf_op jit(solution)/shard_map/ppermute | solution.py:292
  28.8 1.9 %collective-permute-done.4 = f32[2,3712]{1,0:T(2,128)S(1)} collective-permute-done((f32[2,3712]{1,0:T(2,128)S(1)}, f32[2,3712]{1,0:T(2,128)S(1)}, u32[]{:S(2)}, u32[]{:S(2)}) %collective-permute-start.4) | collective-permute-done | bytes 29728 | tf_op jit(solution)/shard_map/ppermute | solution.py:292
  30.8 0.1 collective-permute-start.5
  30.9 1.2 %collective-permute-done.5 = f32[2,2816]{1,0:T(2,128)S(1)} collective-permute-done((f32[2,2816]{1,0:T(2,128)S(1)}, f32[2,2816]{1,0:T(2,128)S(1)}, u32[]{:S(2)}, u32[]{:S(2)}) %collective-permute-start.5) | collective-permute-done | bytes 22560 | tf_op jit(solution)/shard_map/ppermute | solution.py:292
  32.1 0.1 collective-permute-start.6
  32.2 3.8 %collective-permute-done.6 = f32[2,2816]{1,0:T(2,128)S(1)} collective-permute-done((f32[2,2816]{1,0:T(2,128)S(1)}, f32[2,2816]{1,0:T(2,128)S(1)}, u32[]{:S(2)}, u32[]{:S(2)}) %collective-permute-start.6) | collective-permute-done | bytes 22560 | tf_op jit(solution)/shard_map/ppermute | solution.py:292
  36.1 0.6 %collective-permute-start.7 = (f32[2,2816]{1,0:T(2,128)S(1)}, f32[2,2816]{1,0:T(2,128)S(1)}, u32[]{:S(2)}, u32[]{:S(2)}) collective-permute-start(f32[2,2816]{1,0:T(2,128)S(1)} %pad_maximum_fusion.2), channel_id=1, source_target_pairs={{0,32},{8,40},{16,48},{24,56},{32,0},{40,8},{48,16},{56,24},{64,96... | collective-permute-start | bytes 67592 | tf_op jit(solution)/shard_map/ppermute | solution.py:292
  36.7 3.3 %collective-permute-done.7 = f32[2,2816]{1,0:T(2,128)S(1)} collective-permute-done((f32[2,2816]{1,0:T(2,128)S(1)}, f32[2,2816]{1,0:T(2,128)S(1)}, u32[]{:S(2)}, u32[]{:S(2)}) %collective-permute-start.7) | collective-permute-done | bytes 22560 | tf_op jit(solution)/shard_map/ppermute | solution.py:292
  40.0 2.0 %collective-permute-start.8 = (f32[2,1792]{1,0:T(2,128)S(1)}, f32[2,1792]{1,0:T(2,128)S(1)}, u32[]{:S(2)}, u32[]{:S(2)}) collective-permute-start(f32[2,1792]{1,0:T(2,128)S(1)} %pad_maximum_fusion.3), channel_id=1, source_target_pairs={{0,96},{8,104},{16,112},{24,120},{32,64},{40,72},{48,80},{56,88},{... | collective-permute-start | bytes 43016 | tf_op jit(solution)/shard_map/ppermute | solution.py:292
  42.1 3.0 %collective-permute-done.8 = f32[2,1792]{1,0:T(2,128)S(1)} collective-permute-done((f32[2,1792]{1,0:T(2,128)S(1)}, f32[2,1792]{1,0:T(2,128)S(1)}, u32[]{:S(2)}, u32[]{:S(2)}) %collective-permute-start.8) | collective-permute-done | bytes 14368 | tf_op jit(solution)/shard_map/ppermute | solution.py:292
  45.1 0.0 copy-done
  45.1 0.0 copy-done.1
  45.1 0.8 %shard_map.59 = (f32[2,2048]{1,0:T(2,128)}, f32[2,512]{1,0:T(2,128)}, f32[1]{0:T(128)}) custom-call(f32[2,768]{1,0:T(2,128)S(1)} %pad_maximum_fusion.4.sums, f32[2,3072]{1,0:T(2,128)S(1)} %get-tuple-element.15.grads, f32[2,1024]{1,0:T(2,128)S(1)} %get-tuple-element.8.low_add, f32[2,1024]{1,0:T(2,128)S(1)} %get-tuple-element.7.high_add, ...), custom_call_target="tpu_custom_call" | custom-call | tf_op jit(solution)/shard_map/pallas_call | solution.py:270
  (28 shorter events, 0.3 us)
Async XLA Ops:
  0.6 44.5 %copy-start = (f32[2,2048]{1,0:T(2,128)S(1)}, f32[2,2048]{1,0:T(2,128)}, u32[]{:S(2)}) copy-start(f32[2,2048]{1,0:T(2,128)} %filt.1) | copy-start | bytes 49156
  0.6 44.5 %copy-start.1 = (f32[2,512]{1,0:T(2,128)S(1)}, f32[2,512]{1,0:T(2,128)}, u32[]{:S(2)}) copy-start(f32[2,512]{1,0:T(2,128)} %prof.1) | copy-start | bytes 12292
  0.7 5.6 %collective-permute-start = (f32[2,2048]{1,0:T(2,128)}, f32[2,2048]{1,0:T(2,128)S(1)}, u32[]{:S(2)}, u32[]{:S(2)}) collective-permute-start(f32[2,2048]{1,0:T(2,128)} %filt.1), channel_id=1, source_target_pairs={{0,8},{8,16},{16,24},{24,32},{32,40},{40,48},{48,56},{56,64},{64,7... | collective-permute-start | bytes 49160 | tf_op jit(solution)/shard_map/ppermute | solution.py:299
  0.7 5.6 %collective-permute-start.1 = (f32[2,2048]{1,0:T(2,128)}, f32[2,2048]{1,0:T(2,128)S(1)}, u32[]{:S(2)}, u32[]{:S(2)}) collective-permute-start(f32[2,2048]{1,0:T(2,128)} %filt.1), channel_id=1, source_target_pairs={{8,0},{16,8},{24,16},{32,24},{40,32},{48,40},{56,48},{64,56},{72,6... | collective-permute-start | bytes 49160 | tf_op jit(solution)/shard_map/ppermute | solution.py:299
  15.7 4.0 %collective-permute-start.2 = (f32[2,3712]{1,0:T(2,128)S(1)}, f32[2,3712]{1,0:T(2,128)S(1)}, u32[]{:S(2)}, u32[]{:S(2)}) collective-permute-start(f32[2,3712]{1,0:T(2,128)S(1)} %shard_map.58), channel_id=1, source_target_pairs={{0,2},{1,3},{2,0},{3,1},{4,6},{5,7},{6,4},{7,5},{8,10},{9,11},{10,... | collective-permute-start | bytes 89096 | tf_op jit(solution)/shard_map/ppermute | solution.py:292
  19.7 5.2 %collective-permute-start.3 = (f32[2,3712]{1,0:T(2,128)S(1)}, f32[2,3712]{1,0:T(2,128)S(1)}, u32[]{:S(2)}, u32[]{:S(2)}) collective-permute-start(f32[2,3712]{1,0:T(2,128)S(1)} %add.186), channel_id=1, source_target_pairs={{0,6},{1,7},{2,4},{3,5},{4,2},{5,3},{6,0},{7,1},{8,14},{9,15},{10,... | collective-permute-start | bytes 89096 | tf_op jit(solution)/shard_map/ppermute | solution.py:292
  24.9 5.8 %collective-permute-start.4 = (f32[2,3712]{1,0:T(2,128)S(1)}, f32[2,3712]{1,0:T(2,128)S(1)}, u32[]{:S(2)}, u32[]{:S(2)}) collective-permute-start(f32[2,3712]{1,0:T(2,128)S(1)} %add.187), channel_id=1, source_target_pairs={{0,1},{1,0},{2,3},{3,2},{4,5},{5,4},{6,7},{7,6},{8,9},{9,8},{10,11... | collective-permute-start | bytes 89096 | tf_op jit(solution)/shard_map/ppermute | solution.py:292
  30.8 1.3 %collective-permute-start.5 = (f32[2,2816]{1,0:T(2,128)S(1)}, f32[2,2816]{1,0:T(2,128)S(1)}, u32[]{:S(2)}, u32[]{:S(2)}) collective-permute-start(f32[2,2816]{1,0:T(2,128)S(1)} %pad_maximum_fusion), channel_id=1, source_target_pairs={{0,8},{8,0},{16,24},{24,16},{32,40},{40,32},{48,56},{56,48},{64,72... | collective-permute-start | bytes 67592 | tf_op jit(solution)/shard_map/ppermute | solution.py:292
  32.1 3.9 %collective-permute-start.6 = (f32[2,2816]{1,0:T(2,128)S(1)}, f32[2,2816]{1,0:T(2,128)S(1)}, u32[]{:S(2)}, u32[]{:S(2)}) collective-permute-start(f32[2,2816]{1,0:T(2,128)S(1)} %pad_maximum_fusion.1), channel_id=1, source_target_pairs={{0,16},{8,24},{16,0},{24,8},{32,48},{40,56},{48,32},{56,40},{64,80... | collective-permute-start | bytes 67592 | tf_op jit(solution)/shard_map/ppermute | solution.py:292
  36.1 3.9 %collective-permute-start.7 = (f32[2,2816]{1,0:T(2,128)S(1)}, f32[2,2816]{1,0:T(2,128)S(1)}, u32[]{:S(2)}, u32[]{:S(2)}) collective-permute-start(f32[2,2816]{1,0:T(2,128)S(1)} %pad_maximum_fusion.2), channel_id=1, source_target_pairs={{0,32},{8,40},{16,48},{24,56},{32,0},{40,8},{48,16},{56,24},{64,96... | collective-permute-start | bytes 67592 | tf_op jit(solution)/shard_map/ppermute | solution.py:292
  40.0 5.0 %collective-permute-start.8 = (f32[2,1792]{1,0:T(2,128)S(1)}, f32[2,1792]{1,0:T(2,128)S(1)}, u32[]{:S(2)}, u32[]{:S(2)}) collective-permute-start(f32[2,1792]{1,0:T(2,128)S(1)} %pad_maximum_fusion.3), channel_id=1, source_target_pairs={{0,96},{8,104},{16,112},{24,120},{32,64},{40,72},{48,80},{56,88},{... | collective-permute-start | bytes 43016 | tf_op jit(solution)/shard_map/ppermute | solution.py:292

commit v6 on v5

--- a/solution.py
+++ b/solution.py
@@ -122,7 +122,7 @@
             mag = size[krows, :]
             a_re = jnp.zeros((GROUP, LANES), jnp.float32)
             a_im = jnp.zeros((GROUP, LANES), jnp.float32)
-            e_sum = jnp.zeros((GROUP, LANES), jnp.float32)
+            e_sum = err[...]
             for tile in range(tiles):
                 cols = pl.ds(tile * LANES, LANES)
                 above = pl.ds((edge + tile + q) * LANES, LANES)
@@ -165,7 +165,7 @@
                     down_im[rows, below] += d_im
             part_re[krows, :] = a_re
             part_im[krows, :] = a_im
-            err[...] += e_sum
+            err[...] = e_sum
             return carry
 
         lax.fori_loop(0, ROWS // GROUP, group, 0, unroll=UNROLL)
@@ -200,16 +200,20 @@
         out[row, 0:halo] = fall[:, :halo] * keep_low
         out[row, halo : halo + owned] = fall[:, halo:] + rise[:, :owned]
         out[row, halo + owned : width] = rise[:, owned:] * keep_high
-    turned = [
-        lax.dot_general(
-            ones,
-            sums[...],
-            (((1,), (1,)), ((), ())),
-            precision=lax.Precision.HIGHEST,
-            preferred_element_type=jnp.float32,
-        )[0:1, :]
-        for sums in (part_re, part_im)
-    ]
+    turned = []
+    for sums in (part_re, part_im):
+        rest = sums[...]
+        line = jnp.zeros((8, harmonics), jnp.float32)
+        for _ in range(3):
+            term = rest.astype(jnp.bfloat16)
+            rest = rest - term.astype(jnp.float32)
+            line = line + lax.dot_general(
+                ones.astype(jnp.bfloat16),
+                term,
+                (((1,), (1,)), ((), ())),
+                preferred_element_type=jnp.float32,
+            )
+        turned.append(line[0:1, :])
     line = turned[0] * turn_re - turned[1] * turn_im
     out[0:1, width : width + harmonics] = factor * line
     line = turned[0] * turn_im + turned[1] * turn_re

time: 46.1 us -> 46 us (level)
  no operation moved by 1% of the time
where the time goes in v6:
time: 46 us; the launch traced here: 45.8 us
  waiting for transfers between devices  18 us (39%)
  starting transfers between devices  15.2 us (33%)
  Pallas kernels  9.98 us (22%)
  other arithmetic  1.74 us (4%)
  between operations  0.83 us (2%)
    ppermute x7, waiting for transfers between devices, swap(): return lax.ppermute(values, axis, [(i, i ^ mask) for i in range(count)])  17.8 us
    ppermute x7, starting transfers between devices, swap(): return lax.ppermute(values, axis, [(i, i ^ mask) for i in range(count)])  11.2 us
    pallas_call x1, Pallas kernels, local_gradients(): pl.pallas_call(functools.partial(gradient_kernel, factor), in_specs=[anyw...  9.22 us
    ppermute x1, starting transfers between devices, neighbours(): lax.ppermute(to_previous, axis, back)  3.96 us
  transfers between devices with their start and end apart: 9, of which 9 were waited for; matrix products, arithmetic and copies ran while one was open for 3% of the time, Pallas kernels for 0%

profile of v6, /device:TPU:0, one launch (start us, length us, event | category | flops | bytes accessed | tf_op | source)
XLA Modules:
  0.0 45.8 jit_solution(4208100201275169415)
XLA Ops:
  0.6 0.0 copy-start
  0.6 0.0 copy-start.1
  0.7 0.1 collective-permute-start
  0.7 4.0 %collective-permute-start.1 = (f32[2,2048]{1,0:T(2,128)}, f32[2,2048]{1,0:T(2,128)S(1)}, u32[]{:S(2)}, u32[]{:S(2)}) collective-permute-start(f32[2,2048]{1,0:T(2,128)} %filt.1), channel_id=1, source_target_pairs={{8,0},{16,8},{24,16},{32,24},{40,32},{48,40},{56,48},{64,56},{72,6... | collective-permute-start | bytes 49160 | tf_op jit(solution)/shard_map/ppermute | solution.py:303
  4.7 0.8 %broadcast_multiply_fusion.own = f32[2,2048]{1,0:T(2,128)S(1)} fusion(f32[2,2048]{1,0:T(2,128)} %filt.1, f32[]{:T(128)S(6)} %select_n.114), kind=kLoop, calls=%fused_computation.10 | loop fusion | flops 4096 | bytes 32772 | tf_op jit(solution)/shard_map/mul | solution.py:340
  5.5 0.7 %broadcast_multiply_fusion.1.prof = f32[2,512]{1,0:T(2,128)S(1)} fusion(f32[2,512]{1,0:T(2,128)} %prof.1, f32[]{:T(128)S(6)} %select_n.114), kind=kLoop, calls=%fused_computation.24 | loop fusion | flops 1024 | bytes 8196 | tf_op jit(solution)/shard_map/mul | solution.py:341
  6.1 0.1 collective-permute-done.prev
  6.2 0.1 collective-permute-done.1.after
  6.3 9.2 %shard_map.58 = f32[2,3712]{1,0:T(2,128)S(1)} custom-call(bf16[1,2,512,2048]{3,2,1,0:T(8,128)(2,1)} %spectra.1, f32[2,512]{1,0:T(2,128)S(1)} %broadcast_multiply_fusion.1.prof, f32[2,2048]{1,0:T(2,128)S(1)} %broadcast_multiply_fusion.own, f32[2,2048]{1,0:T(2,128)S(1)} %collective-permute-done.prev, f32[2,2048]{1,0:T(2,128)S(1)} %collective-permute-done.1.after), custom_call_target="tpu_custom_call" | custom-call | tf_op jit(solution)/shard_map/pallas_call | solution.py:233
  15.6 1.6 %collective-permute-start.2 = (f32[2,3712]{1,0:T(2,128)S(1)}, f32[2,3712]{1,0:T(2,128)S(1)}, u32[]{:S(2)}, u32[]{:S(2)}) collective-permute-start(f32[2,3712]{1,0:T(2,128)S(1)} %shard_map.58), channel_id=1, source_target_pairs={{0,2},{1,3},{2,0},{3,1},{4,6},{5,7},{6,4},{7,5},{8,10},{9,11},{10,... | collective-permute-start | bytes 89096 | tf_op jit(solution)/shard_map/ppermute | solution.py:296
  17.1 2.4 %collective-permute-done.2 = f32[2,3712]{1,0:T(2,128)S(1)} collective-permute-done((f32[2,3712]{1,0:T(2,128)S(1)}, f32[2,3712]{1,0:T(2,128)S(1)}, u32[]{:S(2)}, u32[]{:S(2)}) %collective-permute-start.2) | collective-permute-done | bytes 29728 | tf_op jit(solution)/shard_map/ppermute | solution.py:296
  19.6 2.8 %collective-permute-start.3 = (f32[2,3712]{1,0:T(2,128)S(1)}, f32[2,3712]{1,0:T(2,128)S(1)}, u32[]{:S(2)}, u32[]{:S(2)}) collective-permute-start(f32[2,3712]{1,0:T(2,128)S(1)} %add.186), channel_id=1, source_target_pairs={{0,6},{1,7},{2,4},{3,5},{4,2},{5,3},{6,0},{7,1},{8,14},{9,15},{10,... | collective-permute-start | bytes 89096 | tf_op jit(solution)/shard_map/ppermute | solution.py:296
  22.4 2.3 %collective-permute-done.3 = f32[2,3712]{1,0:T(2,128)S(1)} collective-permute-done((f32[2,3712]{1,0:T(2,128)S(1)}, f32[2,3712]{1,0:T(2,128)S(1)}, u32[]{:S(2)}, u32[]{:S(2)}) %collective-permute-start.3) | collective-permute-done | bytes 29728 | tf_op jit(solution)/shard_map/ppermute | solution.py:296
  24.8 3.9 %collective-permute-start.4 = (f32[2,3712]{1,0:T(2,128)S(1)}, f32[2,3712]{1,0:T(2,128)S(1)}, u32[]{:S(2)}, u32[]{:S(2)}) collective-permute-start(f32[2,3712]{1,0:T(2,128)S(1)} %add.187), channel_id=1, source_target_pairs={{0,1},{1,0},{2,3},{3,2},{4,5},{5,4},{6,7},{7,6},{8,9},{9,8},{10,11... | collective-permute-start | bytes 89096 | tf_op jit(solution)/shard_map/ppermute | solution.py:296
  28.7 1.9 %collective-permute-done.4 = f32[2,3712]{1,0:T(2,128)S(1)} collective-permute-done((f32[2,3712]{1,0:T(2,128)S(1)}, f32[2,3712]{1,0:T(2,128)S(1)}, u32[]{:S(2)}, u32[]{:S(2)}) %collective-permute-start.4) | collective-permute-done | bytes 29728 | tf_op jit(solution)/shard_map/ppermute | solution.py:296
  30.6 0.1 collective-permute-start.5
  30.7 1.2 %collective-permute-done.5 = f32[2,2816]{1,0:T(2,128)S(1)} collective-permute-done((f32[2,2816]{1,0:T(2,128)S(1)}, f32[2,2816]{1,0:T(2,128)S(1)}, u32[]{:S(2)}, u32[]{:S(2)}) %collective-permute-start.5) | collective-permute-done | bytes 22560 | tf_op jit(solution)/shard_map/ppermute | solution.py:296
  32.0 0.1 collective-permute-start.6
  32.1 3.8 %collective-permute-done.6 = f32[2,2816]{1,0:T(2,128)S(1)} collective-permute-done((f32[2,2816]{1,0:T(2,128)S(1)}, f32[2,2816]{1,0:T(2,128)S(1)}, u32[]{:S(2)}, u32[]{:S(2)}) %collective-permute-start.6) | collective-permute-done | bytes 22560 | tf_op jit(solution)/shard_map/ppermute | solution.py:296
  36.0 0.6 %collective-permute-start.7 = (f32[2,2816]{1,0:T(2,128)S(1)}, f32[2,2816]{1,0:T(2,128)S(1)}, u32[]{:S(2)}, u32[]{:S(2)}) collective-permute-start(f32[2,2816]{1,0:T(2,128)S(1)} %pad_maximum_fusion.2), channel_id=1, source_target_pairs={{0,32},{8,40},{16,48},{24,56},{32,0},{40,8},{48,16},{56,24},{64,96... | collective-permute-start | bytes 67592 | tf_op jit(solution)/shard_map/ppermute | solution.py:296
  36.6 3.3 %collective-permute-done.7 = f32[2,2816]{1,0:T(2,128)S(1)} collective-permute-done((f32[2,2816]{1,0:T(2,128)S(1)}, f32[2,2816]{1,0:T(2,128)S(1)}, u32[]{:S(2)}, u32[]{:S(2)}) %collective-permute-start.7) | collective-permute-done | bytes 22560 | tf_op jit(solution)/shard_map/ppermute | solution.py:296
  39.9 2.0 %collective-permute-start.8 = (f32[2,1792]{1,0:T(2,128)S(1)}, f32[2,1792]{1,0:T(2,128)S(1)}, u32[]{:S(2)}, u32[]{:S(2)}) collective-permute-start(f32[2,1792]{1,0:T(2,128)S(1)} %pad_maximum_fusion.3), channel_id=1, source_target_pairs={{0,96},{8,104},{16,112},{24,120},{32,64},{40,72},{48,80},{56,88},{... | collective-permute-start | bytes 43016 | tf_op jit(solution)/shard_map/ppermute | solution.py:296
  42.0 3.0 %collective-permute-done.8 = f32[2,1792]{1,0:T(2,128)S(1)} collective-permute-done((f32[2,1792]{1,0:T(2,128)S(1)}, f32[2,1792]{1,0:T(2,128)S(1)}, u32[]{:S(2)}, u32[]{:S(2)}) %collective-permute-start.8) | collective-permute-done | bytes 14368 | tf_op jit(solution)/shard_map/ppermute | solution.py:296
  45.0 0.0 copy-done
  45.0 0.0 copy-done.1
  45.0 0.8 %shard_map.59 = (f32[2,2048]{1,0:T(2,128)}, f32[2,512]{1,0:T(2,128)}, f32[1]{0:T(128)}) custom-call(f32[2,768]{1,0:T(2,128)S(1)} %pad_maximum_fusion.4.sums, f32[2,3072]{1,0:T(2,128)S(1)} %get-tuple-element.15.grads, f32[2,1024]{1,0:T(2,128)S(1)} %get-tuple-element.8.low_add, f32[2,1024]{1,0:T(2,128)S(1)} %get-tuple-element.7.high_add, ...), custom_call_target="tpu_custom_call" | custom-call | tf_op jit(solution)/shard_map/pallas_call | solution.py:274
  (28 shorter events, 0.3 us)
Async XLA Ops:
  0.6 44.4 %copy-start = (f32[2,2048]{1,0:T(2,128)S(1)}, f32[2,2048]{1,0:T(2,128)}, u32[]{:S(2)}) copy-start(f32[2,2048]{1,0:T(2,128)} %filt.1) | copy-start | bytes 49156
  0.6 44.4 %copy-start.1 = (f32[2,512]{1,0:T(2,128)S(1)}, f32[2,512]{1,0:T(2,128)}, u32[]{:S(2)}) copy-start(f32[2,512]{1,0:T(2,128)} %prof.1) | copy-start | bytes 12292
  0.7 5.6 %collective-permute-start = (f32[2,2048]{1,0:T(2,128)}, f32[2,2048]{1,0:T(2,128)S(1)}, u32[]{:S(2)}, u32[]{:S(2)}) collective-permute-start(f32[2,2048]{1,0:T(2,128)} %filt.1), channel_id=1, source_target_pairs={{0,8},{8,16},{16,24},{24,32},{32,40},{40,48},{48,56},{56,64},{64,7... | collective-permute-start | bytes 49160 | tf_op jit(solution)/shard_map/ppermute | solution.py:303
  0.7 5.6 %collective-permute-start.1 = (f32[2,2048]{1,0:T(2,128)}, f32[2,2048]{1,0:T(2,128)S(1)}, u32[]{:S(2)}, u32[]{:S(2)}) collective-permute-start(f32[2,2048]{1,0:T(2,128)} %filt.1), channel_id=1, source_target_pairs={{8,0},{16,8},{24,16},{32,24},{40,32},{48,40},{56,48},{64,56},{72,6... | collective-permute-start | bytes 49160 | tf_op jit(solution)/shard_map/ppermute | solution.py:303
  15.6 4.0 %collective-permute-start.2 = (f32[2,3712]{1,0:T(2,128)S(1)}, f32[2,3712]{1,0:T(2,128)S(1)}, u32[]{:S(2)}, u32[]{:S(2)}) collective-permute-start(f32[2,3712]{1,0:T(2,128)S(1)} %shard_map.58), channel_id=1, source_target_pairs={{0,2},{1,3},{2,0},{3,1},{4,6},{5,7},{6,4},{7,5},{8,10},{9,11},{10,... | collective-permute-start | bytes 89096 | tf_op jit(solution)/shard_map/ppermute | solution.py:296
  19.6 5.2 %collective-permute-start.3 = (f32[2,3712]{1,0:T(2,128)S(1)}, f32[2,3712]{1,0:T(2,128)S(1)}, u32[]{:S(2)}, u32[]{:S(2)}) collective-permute-start(f32[2,3712]{1,0:T(2,128)S(1)} %add.186), channel_id=1, source_target_pairs={{0,6},{1,7},{2,4},{3,5},{4,2},{5,3},{6,0},{7,1},{8,14},{9,15},{10,... | collective-permute-start | bytes 89096 | tf_op jit(solution)/shard_map/ppermute | solution.py:296
  24.8 5.8 %collective-permute-start.4 = (f32[2,3712]{1,0:T(2,128)S(1)}, f32[2,3712]{1,0:T(2,128)S(1)}, u32[]{:S(2)}, u32[]{:S(2)}) collective-permute-start(f32[2,3712]{1,0:T(2,128)S(1)} %add.187), channel_id=1, source_target_pairs={{0,1},{1,0},{2,3},{3,2},{4,5},{5,4},{6,7},{7,6},{8,9},{9,8},{10,11... | collective-permute-start | bytes 89096 | tf_op jit(solution)/shard_map/ppermute | solution.py:296
  30.6 1.3 %collective-permute-start.5 = (f32[2,2816]{1,0:T(2,128)S(1)}, f32[2,2816]{1,0:T(2,128)S(1)}, u32[]{:S(2)}, u32[]{:S(2)}) collective-permute-start(f32[2,2816]{1,0:T(2,128)S(1)} %pad_maximum_fusion), channel_id=1, source_target_pairs={{0,8},{8,0},{16,24},{24,16},{32,40},{40,32},{48,56},{56,48},{64,72... | collective-permute-start | bytes 67592 | tf_op jit(solution)/shard_map/ppermute | solution.py:296
  32.0 3.9 %collective-permute-start.6 = (f32[2,2816]{1,0:T(2,128)S(1)}, f32[2,2816]{1,0:T(2,128)S(1)}, u32[]{:S(2)}, u32[]{:S(2)}) collective-permute-start(f32[2,2816]{1,0:T(2,128)S(1)} %pad_maximum_fusion.1), channel_id=1, source_target_pairs={{0,16},{8,24},{16,0},{24,8},{32,48},{40,56},{48,32},{56,40},{64,80... | collective-permute-start | bytes 67592 | tf_op jit(solution)/shard_map/ppermute | solution.py:296
  36.0 3.9 %collective-permute-start.7 = (f32[2,2816]{1,0:T(2,128)S(1)}, f32[2,2816]{1,0:T(2,128)S(1)}, u32[]{:S(2)}, u32[]{:S(2)}) collective-permute-start(f32[2,2816]{1,0:T(2,128)S(1)} %pad_maximum_fusion.2), channel_id=1, source_target_pairs={{0,32},{8,40},{16,48},{24,56},{32,0},{40,8},{48,16},{56,24},{64,96... | collective-permute-start | bytes 67592 | tf_op jit(solution)/shard_map/ppermute | solution.py:296
  39.9 5.0 %collective-permute-start.8 = (f32[2,1792]{1,0:T(2,128)S(1)}, f32[2,1792]{1,0:T(2,128)S(1)}, u32[]{:S(2)}, u32[]{:S(2)}) collective-permute-start(f32[2,1792]{1,0:T(2,128)S(1)} %pad_maximum_fusion.3), channel_id=1, source_target_pairs={{0,96},{8,104},{16,112},{24,120},{32,64},{40,72},{48,80},{56,88},{... | collective-permute-start | bytes 43016 | tf_op jit(solution)/shard_map/ppermute | solution.py:296
